TPU v7x, 32 devices: a whole 2x2x4 slice. The times are simulated.
32 devices in a mesh: dp: 8 (over z, y), tensor: 4 (over x, core).
Axes of the slice: x: 2, y: 2, z: 4, core: 2. Of those that a mesh axis runs over, the one named last changes fastest.
Arguments:
- inputs: bfloat16 [4096, 5120], P('dp', 'tensor'), may hold values from -6 to 6
- cotangent: bfloat16 [4096, 1024], P('dp', 'tensor'), may hold values from -1.5 to 1.5
- base_weight: bfloat16 [5120, 1024], P('tensor'), may hold values from -0.078125 to 0.078125
- down_a: bfloat16 [16, 5120, 16], P('dp', 'tensor'), may hold values from -0.078125 to 0.078125
- up_b: bfloat16 [16, 16, 1024], P('dp', None, 'tensor'), may hold values from -1.5 to 1.5
- block_adapter: int32 [32], P('dp'), may hold values from 0 to 15, as said below
- token_adapter: int32 [4096], P('dp'), may hold values from -1 to 15, as said below
- owner_map: int32 [16], replicated, may hold values from 0 to 15, each once
Outputs:
- gradient_wrt_input: bfloat16 [4096, 5120], P('dp', 'tensor')
- grad_b: float32 [16, 16, 1024], P('dp', None, 'tensor')
Inputs may be any that keep to these rules, and one draw needn't show every extreme that they name: `block_adapter`: each block of 128 rows serves one adapter; some adapters serve many blocks. `token_adapter`: in each block the first rows (at least 32 of them) carry the block's adapter and the rest are padding with -1. A permutation; adapter e stands at slot owner_map[e], on dp index owner_map[e] // 2.
All inputs are finite; a program needn't handle non-finite values.
Results may differ from a plain program's by a relative error of at most 0.0045.
Values may be sent and summed in bfloat16 or wider, within the bound.
A program may use at most 64 MiB of HBM per device.

v0:
```python
import jax
import jax.numpy as jnp
from jax import lax
from jax.sharding import PartitionSpec as P

adapter_scale_factor = 2.0


def slot_match(slot_ids, row_span, dtype):
    columns = jnp.arange(row_span, dtype=jnp.int32)
    return (slot_ids[:, None] == columns[None, :]).astype(dtype)


def on_device(
    inputs, cotangent, base_weight, down_a, up_b, block_adapter, token_adapter, owner_map
):
    row_count, dpiece = inputs.shape
    kpiece = cotangent.shape[1]
    block_count = block_adapter.shape[0]
    blk_rows = row_count // block_count
    nadapt = owner_map.shape[0]
    own_slots = down_a.shape[0]
    matches = block_adapter[:, None] == jnp.arange(nadapt, dtype=jnp.int32)[None, :]
    slot_ids = jnp.sum(jnp.where(matches, owner_map[None, :], 0), axis=1)
    live_rows = (token_adapter >= 0).astype(jnp.float32)[:, None]
    masked_rows = (cotangent.astype(jnp.float32) * live_rows).astype(jnp.bfloat16)
    input_row_blocks = inputs.reshape(block_count, blk_rows, dpiece)
    g_blocks = masked_rows.reshape(block_count, blk_rows, kpiece)
    shard_piece = lax.all_gather(down_a, "dp", axis=0, tiled=True)
    onehot = slot_match(slot_ids, shard_piece.shape[0], jnp.bfloat16)
    chosen = jnp.einsum("bk,kdr->bdr", onehot, shard_piece, preferred_element_type=jnp.float32)
    selected_down_matrix = chosen.astype(jnp.bfloat16)
    shard_piece = lax.all_gather(up_b, "dp", axis=0, tiled=True)
    onehot = slot_match(slot_ids, shard_piece.shape[0], jnp.bfloat16)
    chosen = jnp.einsum("bk,kro->bro", onehot, shard_piece, preferred_element_type=jnp.float32)
    up_sel = chosen.astype(jnp.bfloat16)
    low_rank_portion = jnp.einsum(
        "aon,anj->aoj", input_row_blocks, selected_down_matrix, preferred_element_type=jnp.float32
    )
    backpart = jnp.einsum("bko,bro->bkr", g_blocks, up_sel, preferred_element_type=jnp.float32)
    low_rank_product, hidden_features = lax.psum((low_rank_portion, backpart), "tensor")
    low_rank_product = (low_rank_product * live_rows.reshape(block_count, blk_rows, 1)).astype(
        jnp.bfloat16
    )
    hidden_features = hidden_features.astype(jnp.bfloat16)
    frozen_path_gradient = lax.dot_general(
        lax.all_gather(masked_rows, "tensor", axis=1, tiled=True),
        base_weight,
        (((1,), (1,)), ((), ())),
        preferred_element_type=jnp.float32,
    )
    adapter_path_gradient = jnp.einsum(
        "eay,exy->eax", hidden_features, selected_down_matrix, preferred_element_type=jnp.float32
    ).reshape(row_count, dpiece)
    gradient_wrt_input = (
        frozen_path_gradient + adapter_scale_factor * adapter_path_gradient
    ).astype(jnp.bfloat16)
    block_partial_terms = adapter_scale_factor * jnp.einsum(
        "bkr,bko->bro", low_rank_product, g_blocks, preferred_element_type=jnp.float32
    )
    onehot = slot_match(slot_ids, lax.axis_size("dp") * own_slots, jnp.float32)
    grad_b = lax.psum_scatter(
        jnp.einsum("bj,bro->jro", onehot, block_partial_terms, precision=lax.Precision.HIGHEST),
        "dp",
        scatter_dimension=0,
        tiled=True,
    )
    return (gradient_wrt_input, grad_b)


def solution(mesh):
    in_specs = (
        P("dp", "tensor"),
        P("dp", "tensor"),
        P("tensor", None),
        P("dp", "tensor", None),
        P("dp", None, "tensor"),
        P("dp"),
        P("dp"),
        P(),
    )
    out_specs = (P("dp", "tensor"), P("dp", None, "tensor"))
    return jax.shard_map(
        on_device, mesh=mesh, in_specs=in_specs, out_specs=out_specs, check_vma=False
    )
```

profile of v0, /device:TPU:0, one launch (start us, length us, event | category | flops | bytes accessed | tf_op | source)
XLA Modules:
  0.0 161.7 jit_solution(15866511405763404355)
XLA Ops:
  8.0 0.0 copy-start
  8.0 0.0 all-gather.2.cloned.1.call-start
  8.1 0.8 fusion.12
  8.9 1.8 %multiply_convert_fusion = bf16[512,256]{1,0:T(8,128)(2,1)} fusion(bf16[512,256]{1,0:T(8,128)(2,1)} %param.9, f32[512]{0:T(512)S(1)} %get-tuple-element.7), kind=kLoop, calls=%fused_computation.8 | loop fusion | flops 393216 | bytes 526336 | tf_op jit(solution)/shard_map/convert_element_type | solution.py:26
  10.7 0.0 copy-start.1
  10.7 0.0 all-gather.2.cloned.1.call-update
  10.7 0.0 reduce-scatter.2.cloned.1.call-start
  10.8 32.5 %all_gather.10 = bf16[16,16,256]{2,1,0:T(8,128)(2,1)S(1)} all-gather(bf16[2,16,256]{2,1,0:T(8,128)(2,1)} %param.12), channel_id=1, replica_groups=mesh['dp'=8,'tensor'=4] {'dp'}, dimensions={0}, use_global_device_ids=true | all-gather | bytes 147456 | tf_op jit(solution)/shard_map/all_gather | solution.py:33
  43.3 0.9 select_reduce_fusion
  44.1 0.2 convolution_convert_fusion.1
  44.3 1.1 fusion.7
  45.5 31.6 %all_gather.11 = bf16[16,1280,16]{1,2,0:T(8,128)(2,1)S(1)} all-gather(bf16[2,1280,16]{1,2,0:T(8,128)(2,1)} %param.11), channel_id=1, replica_groups=mesh['dp'=8,'tensor'=4] {'dp'}, dimensions={0}, use_global_device_ids=true | all-gather | bytes 737280 | tf_op jit(solution)/shard_map/all_gather | solution.py:29
  77.1 0.3 convolution_convert_fusion
  77.4 1.8 %convolution_bitcast_fusion = f32[4,128,16]{1,2,0:T(8,128)S(1)} fusion(bf16[4,128,1280]{2,1,0:T(8,128)(2,1)} %bitcast.21, bf16[4,1280,16]{1,0,2:T(4,128)(2,1)S(1)} %convolution_convert_fusion), kind=kOutput, calls=%fused_computation.6 | convolution fusion | flops 20971520 | bytes 1507328 | tf_op jit(solution)/shard_map/aon,anj->aoj/dot_general | solution.py:37
  79.2 10.7 %all-reduce = (bf16[4,128,16]{1,2,0:T(8,128)(2,1)S(1)}, f32[4,128,16]{1,2,0:T(8,128)S(1)}) all-reduce(f32[4,128,16]{1,2,0:T(8,128)S(1)} %fusion.7, f32[4,128,16]{1,2,0:T(8,128)S(1)} %convolution_bitcast_fusion), channel_id=1, replica_groups=mesh['dp'=8,'tensor'=4] {'tensor'}, use_global_device_ids=true, to_apply=%region_1.2 | all-reduce | flops 16384 | bytes 114688 | tf_op jit(solution)/shard_map/psum | solution.py:41
  89.9 0.0 copy-done.1
  89.9 0.2 convolution_multiply_fusion.1
  90.1 0.4 fusion.5
  90.5 0.8 copy.22
  91.3 0.0 reduce-scatter.2.cloned.1.call-update
  91.4 2.1 %convolution_multiply_fusion = f32[4,128,1280]{2,1,0:T(8,128)} fusion(bf16[4,1280,16]{1,0,2:T(4,128)(2,1)S(1)} %convolution_convert_fusion, bf16[4,128,16]{1,2,0:T(8,128)(2,1)S(1)} %get-tuple-element.4), kind=kOutput, calls=%fused_computation | convolution fusion | flops 21626880 | bytes 2801664 | tf_op jit(solution)/shard_map/eay,exy->eax/dot_general | solution.py:52
  93.4 0.0 all-gather.2.cloned.1.call-done
  93.4 0.0 copy-done
  93.4 4.7 %fusion = bf16[512,1280]{1,0:T(8,128)(2,1)} fusion(f32[512,1280]{1,0:T(8,128)} %bitcast.20, bf16[512,1024]{1,0:T(8,128)(2,1)} %all-gather.2.cloned.1.call-done, bf16[1280,1024]{1,0:T(8,128)(2,1)S(1)} %copy-done), kind=kOutput, calls=%fused_computation.2 | convolution fusion | flops 1343488000 | bytes 7602176 | tf_op jit(solution)/shard_map/dot_general | solution.py:46
  98.1 56.2 %reduce-scatter.2.cloned.1.call-done = f32[2,16,256]{2,1,0:T(8,128)} async-done(((f32[16,16,256]{2,1,0:T(8,128)}), f32[2,16,256]{2,1,0:T(8,128)}) %reduce-scatter.2.cloned.1.call-update) | async-done | bytes 32784 | tf_op jit(solution)/shard_map/reduce_scatter | solution.py:62
Async XLA Ops:
  8.0 85.4 %copy-start = (bf16[1280,1024]{1,0:T(8,128)(2,1)S(1)}, bf16[1280,1024]{1,0:T(8,128)(2,1)}, u32[]{:S(2)}) copy-start(bf16[1280,1024]{1,0:T(8,128)(2,1)} %param.10) | copy-start | bytes 7864324
  8.0 85.4 %all-gather.2.cloned.1.call-start = ((), (), s32[]{:S(2)}) async-start(), calls=%async_computation.1 | async-start | bytes 1310720 | tf_op jit(solution)/shard_map/all_gather | solution.py:47
  10.7 79.2 %copy-start.1 = (bf16[512,256]{1,0:T(8,128)(2,1)S(1)}, bf16[512,256]{1,0:T(8,128)(2,1)}, u32[]{:S(2)}) copy-start(bf16[512,256]{1,0:T(8,128)(2,1)} %multiply_convert_fusion) | copy-start | bytes 786436
  10.7 143.6 %reduce-scatter.2.cloned.1.call-start = ((), (), s32[]{:S(2)}) async-start(), calls=%async_computation.2 | async-start | bytes 294912 | tf_op jit(solution)/shard_map/reduce_scatter | solution.py:62
Sparse Core Ops, SparseCore 0:
  11.0 19.5 all-gather.1
Sparse Core Ops, SparseCore 1:
  91.4 62.8 reduce-scatter.1
where the time goes:
time: 162 us
  blocking collectives  74.9 us (46%)
  waiting for transfers between devices  56.2 us (35%)
  between operations  15.5 us (10%)
  matrix products  10.7 us (7%)
  other arithmetic  3.48 us (2%)
    reduce_scatter x1, waiting for transfers between devices, on_device(): lax.psum_scatter(jnp.einsum('bj,bro->jro', onehot, block_partial_terms, p...  56.2 us
    all_gather x1, blocking collectives, on_device(): shard_piece = lax.all_gather(up_b, 'dp', axis=0, tiled=True)  32.5 us
    all_gather x1, blocking collectives, on_device(): shard_piece = lax.all_gather(down_a, 'dp', axis=0, tiled=True)  31.6 us
    psum x1, blocking collectives, on_device(): lax.psum((low_rank_portion, backpart), 'tensor')  10.7 us
    dot_general x1, matrix products, on_device(): lax.dot_general(lax.all_gather(masked_rows, 'tensor', axis=1, tiled=True)...  4.69 us
  transfers between devices with their start and end apart: 2, of which 1 were waited for; matrix products, arithmetic and copies ran while one was open for 8% of the time, Pallas kernels for 0%

commit v1 on v0

v1 whole, which is shorter than its diff:
```python
import functools

import jax
import jax.numpy as jnp
from jax import lax
from jax.experimental import pallas as pl
from jax.experimental.pallas import tpu as pltpu
from jax.sharding import PartitionSpec as P

adapter_scale_factor = 2.0
MESH = pl.DeviceIdType.MESH
LAST = (((1,), (1,)), ((), ()))
FIRST = (((0,), (0,)), ((), ()))


def loop(lo, hi, body):
    if hi - lo <= 8:
        for i in range(lo, hi):
            body(i)
    else:
        lax.fori_loop(lo, hi, lambda i, c: (body(i), c)[1], 0)


def kernel(
    ndp, nten, owner_ref, block_ref, tok_ref, x_ref, g_ref, w_ref, a_ref, u_ref,
    out_ref, grad_ref,
    xv, wv, gall, gm, aall, uall, part, sib, chip, outv, gsend, grecv,
    local_sem, out_sem, a_send, a_recv, g_xsend, g_ssend, g_recv,
    p_send, p_recv, c_send, c_recv, r_send, r_recv,
):
    nblk = block_ref.shape[0]
    rows, dpiece = x_ref.shape
    kpiece = g_ref.shape[1]
    brows = rows // nblk
    own = a_ref.shape[0]
    inner = 2 if ndp % 2 == 0 else 1
    outer = ndp // inner
    nx = nten // 2
    me, t = lax.axis_index("dp"), lax.axis_index("tensor")
    z, y = lax.div(me, inner), lax.rem(me, inner)
    xx, c = lax.div(t, 2), lax.rem(t, 2)
    twin = 2 * xx + 1 - c

    mine = pl.ds(me * own, own)
    local = [
        pltpu.make_async_copy(u_ref, uall.at[mine], local_sem.at[0]),
        pltpu.make_async_copy(a_ref, aall.at[mine], local_sem.at[1]),
        pltpu.make_async_copy(g_ref, gall.at[t], local_sem.at[2]),
        pltpu.make_async_copy(x_ref, xv, local_sem.at[3]),
        pltpu.make_async_copy(w_ref, wv, local_sem.at[4]),
    ]
    for cp in local:
        cp.start()

    barrier = pltpu.get_barrier_semaphore()

    def greet_dp(j):
        pl.semaphore_signal(
            barrier, inc=1, device_id=(lax.rem(me + j, ndp), t), device_id_type=MESH
        )

    def greet_ten(j):
        pl.semaphore_signal(
            barrier, inc=1, device_id=(me, lax.rem(t + j, nten)), device_id_type=MESH
        )

    loop(1, ndp, greet_dp)
    loop(1, nten, greet_ten)
    pl.semaphore_wait(barrier, ndp + nten - 2)

    def hop(src, way, first):
        at = pl.ds(src * own, own)
        if way == 2:
            to = inner * z + 1 - y
        else:
            to = inner * (z + 1 - 2 * way) + y
        return [
            pltpu.make_async_remote_copy(
                src_ref=(ref if first else full.at[at]),
                dst_ref=full.at[at],
                send_sem=a_send.at[i, way, src],
                recv_sem=a_recv.at[i, src],
                device_id=(to, t),
                device_id_type=MESH,
            )
            for i, (ref, full) in enumerate(((a_ref, aall), (u_ref, uall)))
        ]

    def for_ways(fn, ways):
        for way in ways:
            if way == 2:
                if inner == 2:
                    fn(2)
            else:
                ok = z + 1 < outer if way == 0 else z > 0
                pl.when(ok)(functools.partial(fn, way))

    def start_hops(src, ways, first=False):
        def go(way):
            for cp in hop(src, way, first):
                cp.start()

        for_ways(go, ways)

    def wait_hops(src, ways, first=False):
        def go(way):
            for cp in hop(src, way, first):
                cp.wait_send()

        for_ways(go, ways)

    def got_hop(src):
        for cp in hop(src, 0, False):
            cp.wait_recv()

    def line(k, fn):
        pl.when(z - k >= 0)(lambda: fn(inner * (z - k) + y, (0, 2)))
        pl.when(z + k < outer)(lambda: fn(inner * (z + k) + y, (1, 2)))

    def piece(src, i):
        return gall.at[src, pl.ds(i * brows, brows)]

    def g_across(j, i):
        return pltpu.make_async_remote_copy(
            src_ref=g_ref.at[pl.ds(i * brows, brows)],
            dst_ref=piece(t, i),
            send_sem=g_xsend.at[j, i],
            recv_sem=g_recv.at[t, i],
            device_id=(me, 2 * lax.rem(xx + j, nx) + c),
            device_id_type=MESH,
        )

    def g_twin(src, i, first=False):
        return pltpu.make_async_remote_copy(
            src_ref=(g_ref.at[pl.ds(i * brows, brows)] if first else piece(src, i)),
            dst_ref=piece(src, i),
            send_sem=g_ssend.at[src, i],
            recv_sem=g_recv.at[src, i],
            device_id=(me, twin),
            device_id_type=MESH,
        )

    def from_x(j):
        return 2 * lax.rem(xx + j, nx) + c

    start_hops(me, (0, 1, 2), True)
    for i in range(nblk):
        for j in range(1, nx):
            g_across(j, i).start()
        g_twin(t, i, True).start()

    def pass_on(src, ways):
        got_hop(src)
        start_hops(src, ways)

    def pass_g(i):
        for j in range(1, nx):
            g_twin(from_x(j), i).wait_recv()
            g_twin(from_x(j), i).start()

    if outer <= 4:
        for k in range(1, max(outer, nblk + 1)):
            if k < outer:
                line(k, pass_on)
            if k <= nblk:
                pass_g(k - 1)
    else:
        loop(1, outer, lambda k: line(k, pass_on))
        for i in range(nblk):
            pass_g(i)

    live = (tok_ref[...] >= 0).astype(jnp.float32)
    tall = []
    for b in range(nblk):
        lane = live[:, b * brows:(b + 1) * brows]
        col = jnp.broadcast_to(lane, (brows, brows)).T.astype(jnp.bfloat16)
        reps = -(-kpiece // brows)
        tall.append(jnp.concatenate([col] * reps, axis=1)[:, :kpiece])
    slots = [owner_ref[block_ref[b]] for b in range(nblk)]

    for cp in local:
        cp.wait()
    if inner == 2:
        loop(0, outer, lambda k: got_hop(inner * k + 1 - y))

    for b in range(nblk):
        span = slice(b * brows, (b + 1) * brows)
        part[0, :, span] = lax.dot_general(
            aall[slots[b]], xv[span, :], LAST, preferred_element_type=jnp.float32
        )
        part[1, :, span] = lax.dot_general(
            uall[slots[b]], gall[t, span, :], LAST, preferred_element_type=jnp.float32
        )
    to_twin = pltpu.make_async_remote_copy(
        src_ref=part, dst_ref=sib, send_sem=p_send, recv_sem=p_recv,
        device_id=(me, twin), device_id_type=MESH,
    )
    to_twin.start()
    to_twin.wait_recv()
    chip[0] = part[...] + sib[...]

    def to_chip(j):
        return pltpu.make_async_remote_copy(
            src_ref=chip.at[0], dst_ref=chip.at[j],
            send_sem=c_send.at[j], recv_sem=c_recv.at[j],
            device_id=(me, from_x(j)), device_id_type=MESH,
        )

    for j in range(1, nx):
        to_chip(j).start()

    for b in range(nblk):
        span = slice(b * brows, (b + 1) * brows)
        for j in range(1, nx):
            g_twin(2 * lax.rem(xx + j, nx) + 1 - c, b).wait_recv()
        g_twin(twin, b).wait_recv()
        for s in range(nten):
            gm[span, s * kpiece:(s + 1) * kpiece] = gall[s, span, :] * tall[b]

    total = chip[0]
    for j in range(1, nx):
        to_chip(j).wait_recv()
        total = total + chip[j]
    lowrank = (total[0] * live).astype(jnp.bfloat16)
    hidden = (total[1] * live).astype(jnp.bfloat16) * jnp.bfloat16(adapter_scale_factor)

    terms = []
    for b in range(nblk):
        span = slice(b * brows, (b + 1) * brows)
        terms.append(
            adapter_scale_factor
            * jnp.dot(lowrank[:, span], gall[t, span, :], preferred_element_type=jnp.float32)
        )

    def share(owner, s):
        acc = jnp.zeros_like(terms[0])
        for b in range(nblk):
            acc = acc + jnp.where(slots[b] == owner * own + s, terms[b], 0.0)
        return acc

    def to_owner(j):
        return pltpu.make_async_remote_copy(
            src_ref=gsend.at[j], dst_ref=grecv.at[j],
            send_sem=r_send.at[j], recv_sem=r_recv.at[j],
            device_id=(lax.rem(me + j, ndp), t), device_id_type=MESH,
        )

    def scatter(j):
        for s in range(own):
            gsend[j, s] = share(lax.rem(me + j, ndp), s).astype(jnp.bfloat16)
        to_owner(j).start()

    loop(1, ndp, scatter)
    for s in range(own):
        grad_ref[s] = share(me, s)

    tile = 256 if dpiece % 256 == 0 else 128
    outs = []
    for n in range(dpiece // tile):
        cols = slice(n * tile, (n + 1) * tile)
        base = lax.dot_general(gm[...], wv[cols, :], LAST, preferred_element_type=jnp.float32)
        for b in range(nblk):
            span = slice(b * brows, (b + 1) * brows)
            low = lax.dot_general(
                hidden[:, span], aall[slots[b], :, cols], FIRST,
                preferred_element_type=jnp.float32,
            )
            outv[span, cols] = (base[span] + low).astype(jnp.bfloat16)
        cp = pltpu.make_async_copy(outv.at[:, cols], out_ref.at[:, cols], out_sem.at[n])
        cp.start()
        outs.append(cp)

    def gather_grad(j):
        to_owner(j).wait_recv()
        grad_ref[...] += grecv[j].astype(jnp.float32)

    loop(1, ndp, gather_grad)

    for cp in outs:
        cp.wait()
    wait_hops(me, (0, 1, 2), True)
    loop(1, outer, lambda k: line(k, wait_hops))
    for i in range(nblk):
        for j in range(1, nx):
            g_across(j, i).wait_send()
            g_twin(from_x(j), i).wait_send()
        g_twin(t, i, True).wait_send()
    to_twin.wait_send()
    for j in range(1, nx):
        to_chip(j).wait_send()
    loop(1, ndp, lambda j: to_owner(j).wait_send())


def on_device(
    ndp, nten, inputs, cotangent, base_weight, down_a, up_b, block_adapter, token_adapter, owner_map
):
    rows, dpiece = inputs.shape
    kpiece = cotangent.shape[1]
    nblk = block_adapter.shape[0]
    own, rank = up_b.shape[:2]
    slots = own * ndp
    kout = base_weight.shape[1]
    nx = nten // 2
    tile = 256 if dpiece % 256 == 0 else 128
    bf16, f32 = jnp.bfloat16, jnp.float32
    smem = pl.BlockSpec(memory_space=pltpu.SMEM)
    vmem = pl.BlockSpec(memory_space=pltpu.VMEM)
    hbm = pl.BlockSpec(memory_space=pl.ANY)
    dma = pltpu.SemaphoreType.DMA
    return pl.pallas_call(
        functools.partial(kernel, ndp, nten),
        out_shape=(
            jax.ShapeDtypeStruct((rows, dpiece), bf16),
            jax.ShapeDtypeStruct((own, rank, kpiece), f32),
        ),
        in_specs=[smem, smem, vmem, hbm, hbm, hbm, hbm, hbm],
        out_specs=(hbm, vmem),
        scratch_shapes=[
            pltpu.VMEM((rows, dpiece), bf16),
            pltpu.VMEM((dpiece, kout), bf16),
            pltpu.VMEM((nten, rows, kpiece), bf16),
            pltpu.VMEM((rows, kout), bf16),
            pltpu.VMEM((slots, rank, dpiece), bf16),
            pltpu.VMEM((slots, rank, kpiece), bf16),
            pltpu.VMEM((2, rank, rows), f32),
            pltpu.VMEM((2, rank, rows), f32),
            pltpu.VMEM((nx, 2, rank, rows), f32),
            pltpu.VMEM((rows, dpiece), bf16),
            pltpu.VMEM((ndp, own, rank, kpiece), bf16),
            pltpu.VMEM((ndp, own, rank, kpiece), bf16),
            dma((5,)),
            dma((dpiece // tile,)),
            dma((2, 3, ndp)),
            dma((2, ndp)),
            dma((nx, nblk)),
            dma((nten, nblk)),
            dma((nten, nblk)),
            dma,
            dma,
            dma((nx,)),
            dma((nx,)),
            dma((ndp,)),
            dma((ndp,)),
        ],
        cost_estimate=pl.CostEstimate(
            flops=2 * rows * dpiece * (kout + 2 * rank),
            bytes_accessed=2 * (2 * rows * dpiece + dpiece * kout + rows * kpiece),
            transcendentals=0,
        ),
        compiler_params=pltpu.CompilerParams(
            collective_id=0, has_side_effects=True, vmem_limit_bytes=48 * 2**20
        ),
    )(
        owner_map, block_adapter, token_adapter.reshape(1, rows), inputs, cotangent, base_weight,
        jnp.swapaxes(down_a, 1, 2), up_b,
    )


def solution(mesh):
    in_specs = (
        P("dp", "tensor"),
        P("dp", "tensor"),
        P("tensor", None),
        P("dp", "tensor", None),
        P("dp", None, "tensor"),
        P("dp"),
        P("dp"),
        P(),
    )
    out_specs = (P("dp", "tensor"), P("dp", None, "tensor"))
    return jax.shard_map(
        functools.partial(on_device, mesh.shape["dp"], mesh.shape["tensor"]),
        mesh=mesh, in_specs=in_specs, out_specs=out_specs, check_vma=False,
    )
```

time: 162 us -> 41.9 us (0.26)
  blocking collectives: 74.9 us -> 0 us
  waiting for transfers between devices: 56.2 us -> 0 us
  Pallas kernels: 0 us -> 31.6 us
  between operations: 15.5 us -> 0.66 us
  matrix products: 10.7 us -> 0 us
  local copies, waits for them, and re-layouts: 0.86 us -> 9.27 us
  other arithmetic: 3.48 us -> 0 us
    all_gather x2 -> x0, blocking collectives: 64.1 us -> none  [the longest x1 32.5 us: on_device(): shard_piece = lax.all_gather(up_b, 'dp', axis=0, tiled=True)]
    reduce_scatter x1 -> x0, waiting for transfers between devices: 56.2 us -> none  [on_device(): lax.psum_scatter(jnp.einsum('bj,bro->jro', onehot, block_partial_terms, p...]
    pallas_call x0 -> x1, Pallas kernels: none -> 31.6 us  [on_device(): pl.pallas_call(functools.partial(kernel, ndp, nten), out_shape=(jax.Shape...]
    dot_general x8 -> x0, matrix products: 10.7 us -> none  [the longest x1 4.69 us: on_device(): lax.dot_general(lax.all_gather(masked_rows, 'tensor', axis=1, tiled=True)...]
    psum x1 -> x0, blocking collectives: 10.7 us -> none  [on_device(): lax.psum((low_rank_portion, backpart), 'tensor')]
    unnamed x4 -> x18, local copies, waits for them, and re-layouts: 0.01 us -> 9.27 us
    convert_element_type x1 -> x0, other arithmetic: 1.79 us -> none  [on_device(): (cotangent.astype(jnp.float32) * live_rows).astype(jnp.bfloat16)]
  transfers between devices with their start and end apart: 2 -> 0, of which waited for: 1 -> 0; matrix products, arithmetic and copies ran while one was open for 8% -> 0% of each run, Pallas kernels for 0% -> 0%
where the time goes in v1:
time: 41.9 us; the launch traced here: 41.6 us
  Pallas kernels  31.6 us (75%)
  local copies, waits for them, and re-layouts  9.27 us (22%)
  between operations  0.66 us (2%)
    pallas_call x1, Pallas kernels, on_device(): pl.pallas_call(functools.partial(kernel, ndp, nten), out_shape=(jax.Shape...  31.6 us
    unnamed x18, local copies, waits for them, and re-layouts  9.27 us

profile of v1, /device:TPU:0, one launch (start us, length us, event | category | flops | bytes accessed | tf_op | source)
XLA Modules:
  0.0 41.6 jit_solution(17962532939160244689)
XLA Ops:
  0.6 0.0 copy-start
  0.6 1.7 %copy-done = bf16[1280,1024]{1,0:T(8,128)(2,1)S(1)} copy-done((bf16[1280,1024]{1,0:T(8,128)(2,1)S(1)}, bf16[1280,1024]{1,0:T(8,128)(2,1)}, u32[]{:S(2)}) %copy-start) | copy-done | bytes 2621464
  2.4 0.0 copy-start.1
  2.4 1.3 %copy-done.1 = bf16[512,1280]{1,0:T(8,128)(2,1)S(1)} copy-done((bf16[512,1280]{1,0:T(8,128)(2,1)S(1)}, bf16[512,1280]{1,0:T(8,128)(2,1)}, u32[]{:S(2)}) %copy-start.1) | copy-done | bytes 1310744
  3.7 0.0 copy-start.2
  3.7 0.9 %copy-done.2 = bf16[512,256]{1,0:T(8,128)(2,1)S(1)} copy-done((bf16[512,256]{1,0:T(8,128)(2,1)S(1)}, bf16[512,256]{1,0:T(8,128)(2,1)}, u32[]{:S(2)}) %copy-start.2) | copy-done | bytes 262168
  4.6 0.0 copy-start.3
  4.6 0.9 %copy-done.3 = bf16[2,1280,16]{1,2,0:T(8,128)(2,1)S(1)} copy-done((bf16[2,1280,16]{1,2,0:T(8,128)(2,1)S(1)}, bf16[2,1280,16]{1,2,0:T(8,128)(2,1)}, u32[]{:S(2)}) %copy-start.3) | copy-done | bytes 81944
  5.5 0.0 copy-start.4
  5.5 0.7 %copy-done.4 = bf16[2,16,256]{2,1,0:T(8,128)(2,1)S(1)} copy-done((bf16[2,16,256]{2,1,0:T(8,128)(2,1)S(1)}, bf16[2,16,256]{2,1,0:T(8,128)(2,1)}, u32[]{:S(2)}) %copy-start.4) | copy-done | bytes 16408
  6.2 0.0 copy-start.5
  6.2 0.7 %copy-done.5 = s32[512]{0:T(512)S(1)} copy-done((s32[512]{0:T(512)S(1)}, s32[512]{0:T(512)}, u32[]{:S(2)}) %copy-start.5) | copy-done | bytes 2072
  6.9 0.0 copy-start.6
  6.9 0.7 %copy-done.6 = s32[16]{0:T(128)S(1)} copy-done((s32[16]{0:T(128)S(1)}, s32[16]{0:T(128)}, u32[]{:S(2)}) %copy-start.6) | copy-done | bytes 88
  7.6 0.0 copy-start.7
  7.6 0.7 %copy-done.7 = s32[4]{0:T(128)S(1)} copy-done((s32[4]{0:T(128)S(1)}, s32[4]{0:T(128)}, u32[]{:S(2)}) %copy-start.7) | copy-done | bytes 40
  8.2 31.6 %shard_map.95 = (bf16[512,1280]{1,0:T(8,128)(2,1)S(1)}, f32[2,16,256]{2,1,0:T(8,128)S(1)}) custom-call(s32[16]{0:T(128)S(1)} %copy-done.6, s32[4]{0:T(128)S(1)} %copy-done.7, s32[1,512]{1,0:T(1,128)S(1)} %bitcast.3, bf16[512,1280]{1,0:T(8,128)(2,1)S(1)} %copy-done.1, bf16[512,256]{1,0:T(8,128)(2,1)S(1)} %copy-done.2, bf16[1280,1024]{1,0:T(8,128)(2,1)S(1)} %copy-done, ...), custom_call_target="tpu_custom_call" | custom-call | flops 1384120320 | bytes 5505024 | tf_op jit(solution)/shard_map/pallas_call | solution.py:310
  39.9 1.1 %copy.12 = bf16[512,1280]{1,0:T(8,128)(2,1)} copy(bf16[512,1280]{1,0:T(8,128)(2,1)S(1)} %get-tuple-element.4) | data formatting | bytes 2621440
  40.9 0.6 %copy.13 = f32[2,16,256]{2,1,0:T(8,128)} copy(f32[2,16,256]{2,1,0:T(8,128)S(1)} %get-tuple-element.5) | data formatting | bytes 65536
Async XLA Ops:
  0.6 1.7 %copy-start = (bf16[1280,1024]{1,0:T(8,128)(2,1)S(1)}, bf16[1280,1024]{1,0:T(8,128)(2,1)}, u32[]{:S(2)}) copy-start(bf16[1280,1024]{1,0:T(8,128)(2,1)} %w_ref.1) | copy-start | bytes 7864324
  2.4 1.3 %copy-start.1 = (bf16[512,1280]{1,0:T(8,128)(2,1)S(1)}, bf16[512,1280]{1,0:T(8,128)(2,1)}, u32[]{:S(2)}) copy-start(bf16[512,1280]{1,0:T(8,128)(2,1)} %x_ref.1) | copy-start | bytes 3932164
  3.7 0.9 %copy-start.2 = (bf16[512,256]{1,0:T(8,128)(2,1)S(1)}, bf16[512,256]{1,0:T(8,128)(2,1)}, u32[]{:S(2)}) copy-start(bf16[512,256]{1,0:T(8,128)(2,1)} %g_ref.1) | copy-start | bytes 786436
  4.6 0.9 %copy-start.3 = (bf16[2,1280,16]{1,2,0:T(8,128)(2,1)S(1)}, bf16[2,1280,16]{1,2,0:T(8,128)(2,1)}, u32[]{:S(2)}) copy-start(bf16[2,1280,16]{1,2,0:T(8,128)(2,1)} %param.11) | copy-start | bytes 245764
  5.5 0.7 %copy-start.4 = (bf16[2,16,256]{2,1,0:T(8,128)(2,1)S(1)}, bf16[2,16,256]{2,1,0:T(8,128)(2,1)}, u32[]{:S(2)}) copy-start(bf16[2,16,256]{2,1,0:T(8,128)(2,1)} %u_ref.1) | copy-start | bytes 49156
  6.2 0.7 %copy-start.5 = (s32[512]{0:T(512)S(1)}, s32[512]{0:T(512)}, u32[]{:S(2)}) copy-start(s32[512]{0:T(512)} %param.14) | copy-start | bytes 6148
  6.9 0.7 %copy-start.6 = (s32[16]{0:T(128)S(1)}, s32[16]{0:T(128)}, u32[]{:S(2)}) copy-start(s32[16]{0:T(128)} %owner_ref.1) | copy-start | bytes 196
  7.6 0.7 %copy-start.7 = (s32[4]{0:T(128)S(1)}, s32[4]{0:T(128)}, u32[]{:S(2)}) copy-start(s32[4]{0:T(128)} %block_ref.1) | copy-start | bytes 52

commit v2 on v1

v2 whole, which is shorter than its diff:
```python
import functools

import jax
import jax.numpy as jnp
from jax import lax
from jax.experimental import pallas as pl
from jax.experimental.pallas import tpu as pltpu
from jax.sharding import PartitionSpec as P

adapter_scale_factor = 2.0
MESH = pl.DeviceIdType.MESH
LAST = (((1,), (1,)), ((), ()))
FIRST = (((0,), (0,)), ((), ()))


def loop(lo, hi, body):
    if hi - lo <= 8:
        for i in range(lo, hi):
            body(i)
    else:
        lax.fori_loop(lo, hi, lambda i, c: (body(i), c)[1], 0)


def kernel(
    ndp, nten, owner_ref, block_ref, tok_ref, x_ref, g_ref, w_ref, a_ref, u_ref,
    out_ref, grad_ref,
    owner, block, tok, xv, wv, gall, gm, acc, aall, uall, part, outv, gsend, grecv,
    local_sem, w_sem, out_sem, a_send, a_recv, g_send, g_fwd, g_recv,
    p_send, p_recv, r_send, r_recv,
):
    nblk = block_ref.shape[0]
    rows, dpiece = x_ref.shape
    kpiece = g_ref.shape[1]
    brows = rows // nblk
    own = a_ref.shape[0]
    inner = 2 if ndp % 2 == 0 else 1
    outer = ndp // inner
    nx = nten // 2
    tiles, _, tile = acc.shape
    me, t = lax.axis_index("dp"), lax.axis_index("tensor")
    z, y = lax.div(me, inner), lax.rem(me, inner)
    xx, c = lax.div(t, 2), lax.rem(t, 2)

    def ten_of(rel):
        core = c if rel % 2 == 0 else 1 - c
        return 2 * lax.rem(xx + rel // 2, nx) + core

    def place_there(rel):
        return 2 * ((nx - rel // 2) % nx) + rel % 2

    barrier = pltpu.get_barrier_semaphore()

    def greet_dp(j):
        pl.semaphore_signal(
            barrier, inc=1, device_id=(lax.rem(me + j, ndp), t), device_id_type=MESH
        )

    def greet_ten(j):
        pl.semaphore_signal(
            barrier, inc=1, device_id=(me, lax.rem(t + j, nten)), device_id_type=MESH
        )

    loop(1, ndp, greet_dp)
    loop(1, nten, greet_ten)

    mine = pl.ds(me * own, own)
    local = [
        pltpu.make_async_copy(src, dst, local_sem.at[i])
        for i, (src, dst) in enumerate((
            (tok_ref, tok), (g_ref, gall.at[0]), (owner_ref, owner), (block_ref, block),
            (u_ref, uall.at[mine]), (a_ref, aall.at[mine]), (x_ref, xv),
        ))
    ]
    weights = [
        pltpu.make_async_copy(
            w_ref.at[:, pl.ds(pl.multiple_of(ten_of(rel) * kpiece, kpiece), kpiece)],
            wv.at[rel], w_sem.at[rel],
        )
        for rel in range(nten)
    ]
    for cp in local[:2] + weights[:1] + local[2:] + weights[1:]:
        cp.start()
    pl.semaphore_wait(barrier, ndp + nten - 2)

    def hop(src, way, first):
        at = pl.ds(src * own, own)
        if way == 2:
            to = inner * z + 1 - y
        else:
            to = inner * (z + 1 - 2 * way) + y
        return [
            pltpu.make_async_remote_copy(
                src_ref=(ref if first else full.at[at]),
                dst_ref=full.at[at],
                send_sem=a_send.at[i, way, src],
                recv_sem=a_recv.at[i, src],
                device_id=(to, t),
                device_id_type=MESH,
            )
            for i, (ref, full) in enumerate(((a_ref, aall), (u_ref, uall)))
        ]

    def for_ways(fn, ways):
        for way in ways:
            if way == 2:
                if inner == 2:
                    fn(2)
            else:
                ok = z + 1 < outer if way == 0 else z > 0
                pl.when(ok)(functools.partial(fn, way))

    def start_hops(src, ways, first=False):
        def go(way):
            for cp in hop(src, way, first):
                cp.start()

        for_ways(go, ways)

    def wait_hops(src, ways, first=False):
        def go(way):
            for cp in hop(src, way, first):
                cp.wait_send()

        for_ways(go, ways)

    def got_hop(src):
        for cp in hop(src, 0, False):
            cp.wait_recv()

    def line(k, fn):
        pl.when(z - k >= 0)(lambda: fn(inner * (z - k) + y, (0, 2)))
        pl.when(z + k < outer)(lambda: fn(inner * (z + k) + y, (1, 2)))

    def span_of(i):
        return pl.ds(i * brows, brows)

    def g_own(rel, i):
        there = place_there(rel)
        return pltpu.make_async_remote_copy(
            src_ref=g_ref.at[span_of(i)],
            dst_ref=gall.at[there, span_of(i)],
            send_sem=g_send.at[rel, i],
            recv_sem=g_recv.at[there, i],
            device_id=(me, ten_of(rel)),
            device_id_type=MESH,
        )

    def g_pass(j, i):
        return pltpu.make_async_remote_copy(
            src_ref=gall.at[2 * j, span_of(i)],
            dst_ref=gall.at[2 * j + 1, span_of(i)],
            send_sem=g_fwd.at[j, i],
            recv_sem=g_recv.at[2 * j + 1, i],
            device_id=(me, ten_of(1)),
            device_id_type=MESH,
        )

    def g_wait(place, i):
        pltpu.make_async_remote_copy(
            src_ref=gall.at[place, span_of(i)],
            dst_ref=gall.at[place, span_of(i)],
            send_sem=g_send.at[0, i],
            recv_sem=g_recv.at[place, i],
            device_id=(me, ten_of(1)),
            device_id_type=MESH,
        ).wait_recv()

    start_hops(me, (0, 1, 2), True)
    for i in range(nblk):
        for j in range(1, nx):
            g_own(2 * j, i).start()
    for i in range(nblk):
        g_own(1, i).start()

    local[0].wait()
    live = (tok[...] >= 0).astype(jnp.float32)
    tall = []
    for b in range(nblk):
        lane = live[:, b * brows:(b + 1) * brows]
        col = jnp.broadcast_to(lane, (brows, brows)).T.astype(jnp.bfloat16)
        reps = -(-kpiece // brows)
        tall.append(jnp.concatenate([col] * reps, axis=1)[:, :kpiece])

    def mask_piece(rel):
        for b in range(nblk):
            gm[rel, span_of(b), :] = gall[rel, span_of(b), :] * tall[b]

    def multiply(rel):
        weights[rel].wait()

        def one(n, carry):
            cols = pl.ds(pl.multiple_of(n * tile, tile), tile)
            prod = lax.dot_general(
                gm[rel], wv[rel, cols, :], LAST, preferred_element_type=jnp.float32
            )
            if rel == 0:
                acc[n] = prod
            else:
                acc[n] += prod
            return carry

        lax.fori_loop(0, tiles, one, 0)

    local[1].wait()
    mask_piece(0)
    multiply(0)

    def pass_on(src, ways):
        got_hop(src)
        start_hops(src, ways)

    def pass_g(i):
        for j in range(1, nx):
            g_wait(2 * j, i)
            g_pass(j, i).start()

    def twin_piece():
        for i in range(nblk):
            g_wait(1, i)
        mask_piece(1)
        multiply(1)

    if outer <= 4:
        for k in range(1, max(outer, nblk + 1)):
            if k < outer:
                line(k, pass_on)
            if k == 1:
                twin_piece()
            if k <= nblk:
                pass_g(k - 1)
    else:
        loop(1, outer, lambda k: line(k, pass_on))
        twin_piece()
        for i in range(nblk):
            pass_g(i)
    for j in range(1, nx):
        mask_piece(2 * j)

    for cp in local[2:]:
        cp.wait()
    slots = [owner[block[b]] for b in range(nblk)]
    if inner == 2:
        loop(0, outer, lambda k: got_hop(inner * k + 1 - y))

    def to_ten(which, rel):
        return pltpu.make_async_remote_copy(
            src_ref=part.at[which, 0], dst_ref=part.at[which, place_there(rel)],
            send_sem=p_send.at[which, rel], recv_sem=p_recv.at[which, place_there(rel)],
            device_id=(me, ten_of(rel)), device_id_type=MESH,
        )

    def from_ten(which, rel):
        pltpu.make_async_remote_copy(
            src_ref=part.at[which, 0], dst_ref=part.at[which, rel],
            send_sem=p_send.at[which, rel], recv_sem=p_recv.at[which, rel],
            device_id=(me, ten_of(rel)), device_id_type=MESH,
        ).wait_recv()

    for which, (pieces, act) in enumerate(((aall, xv), (uall, gall.at[0]))):
        for b in range(nblk):
            span = slice(b * brows, (b + 1) * brows)
            part[which, 0, :, span] = lax.dot_general(
                pieces[slots[b]], act[span, :], LAST, preferred_element_type=jnp.float32
            )
        for rel in range(nten - 1, 0, -1):
            to_ten(which, rel).start()

    for j in range(1, nx):
        multiply(2 * j)

    def summed(which):
        total = part[which, 0]
        for rel in range(1, nten):
            from_ten(which, rel)
            total = total + part[which, rel]
        return (total * live).astype(jnp.bfloat16)

    lowrank = summed(0)

    terms = []
    for b in range(nblk):
        span = slice(b * brows, (b + 1) * brows)
        terms.append(
            adapter_scale_factor
            * jnp.dot(lowrank[:, span], gm[0, span, :], preferred_element_type=jnp.float32)
        )

    def share(dev, s):
        got = jnp.zeros_like(terms[0])
        for b in range(nblk):
            got = got + jnp.where(slots[b] == dev * own + s, terms[b], 0.0)
        return got

    def to_owner(j):
        return pltpu.make_async_remote_copy(
            src_ref=gsend.at[j], dst_ref=grecv.at[j],
            send_sem=r_send.at[j], recv_sem=r_recv.at[j],
            device_id=(lax.rem(me + j, ndp), t), device_id_type=MESH,
        )

    def scatter(j):
        for s in range(own):
            gsend[j, s] = share(lax.rem(me + j, ndp), s).astype(jnp.bfloat16)
        to_owner(j).start()

    loop(1, ndp, scatter)
    for s in range(own):
        grad_ref[s] = share(me, s)

    for j in range(1, nx):
        for i in range(nblk):
            g_wait(2 * j + 1, i)
        mask_piece(2 * j + 1)
        multiply(2 * j + 1)
    hidden = summed(1) * jnp.bfloat16(adapter_scale_factor)
    outs = []
    for n in range(tiles):
        cols = slice(n * tile, (n + 1) * tile)
        for b in range(nblk):
            span = slice(b * brows, (b + 1) * brows)
            low = lax.dot_general(
                hidden[:, span], aall[slots[b], :, cols], FIRST,
                preferred_element_type=jnp.float32,
            )
            outv[n, span, :] = (acc[n, span, :] + low).astype(jnp.bfloat16)
        cp = pltpu.make_async_copy(outv.at[n], out_ref.at[:, cols], out_sem.at[n])
        cp.start()
        outs.append(cp)

    wait_hops(me, (0, 1, 2), True)
    loop(1, outer, lambda k: line(k, wait_hops))
    for i in range(nblk):
        for j in range(1, nx):
            g_own(2 * j, i).wait_send()
            g_pass(j, i).wait_send()
        g_own(1, i).wait_send()
    for which in range(2):
        for rel in range(1, nten):
            to_ten(which, rel).wait_send()

    def gather_grad(j):
        to_owner(j).wait_recv()
        grad_ref[...] += grecv[j].astype(jnp.float32)

    loop(1, ndp, gather_grad)
    loop(1, ndp, lambda j: to_owner(j).wait_send())
    for cp in outs:
        cp.wait()


def on_device(
    ndp, nten, inputs, cotangent, base_weight, down_a, up_b, block_adapter, token_adapter, owner_map
):
    rows, dpiece = inputs.shape
    kpiece = cotangent.shape[1]
    nblk = block_adapter.shape[0]
    own, rank = up_b.shape[:2]
    slots = own * ndp
    kout = base_weight.shape[1]
    nx = nten // 2
    tile = 256 if dpiece % 256 == 0 else 128
    bf16, f32 = jnp.bfloat16, jnp.float32
    hbm = pl.BlockSpec(memory_space=pltpu.HBM)
    dma = pltpu.SemaphoreType.DMA
    return pl.pallas_call(
        functools.partial(kernel, ndp, nten),
        out_shape=(
            jax.ShapeDtypeStruct((rows, dpiece), bf16),
            jax.ShapeDtypeStruct((own, rank, kpiece), f32),
        ),
        in_specs=[hbm] * 8,
        out_specs=(pl.BlockSpec(memory_space=pl.ANY), pl.BlockSpec(memory_space=pltpu.VMEM)),
        scratch_shapes=[
            pltpu.SMEM(owner_map.shape, jnp.int32),
            pltpu.SMEM((nblk,), jnp.int32),
            pltpu.VMEM((1, rows), jnp.int32),
            pltpu.VMEM((rows, dpiece), bf16),
            pltpu.VMEM((nten, dpiece, kpiece), bf16),
            pltpu.VMEM((nten, rows, kpiece), bf16),
            pltpu.VMEM((nten, rows, kpiece), bf16),
            pltpu.VMEM((dpiece // tile, rows, tile), f32),
            pltpu.VMEM((slots, rank, dpiece), bf16),
            pltpu.VMEM((slots, rank, kpiece), bf16),
            pltpu.VMEM((2, nten, rank, rows), f32),
            pltpu.VMEM((dpiece // tile, rows, tile), bf16),
            pltpu.VMEM((ndp, own, rank, kpiece), bf16),
            pltpu.VMEM((ndp, own, rank, kpiece), bf16),
            dma((7,)),
            dma((nten,)),
            dma((dpiece // tile,)),
            dma((2, 3, ndp)),
            dma((2, ndp)),
            dma((nten, nblk)),
            dma((nx, nblk)),
            dma((nten, nblk)),
            dma((2, nten)),
            dma((2, nten)),
            dma((ndp,)),
            dma((ndp,)),
        ],
        cost_estimate=pl.CostEstimate(
            flops=2 * rows * dpiece * (kout + 2 * rank),
            bytes_accessed=2 * (2 * rows * dpiece + dpiece * kout + rows * kpiece),
            transcendentals=0,
        ),
        compiler_params=pltpu.CompilerParams(
            collective_id=0, has_side_effects=True, vmem_limit_bytes=64 * 2**20 - 2**18
        ),
    )(
        owner_map, block_adapter, token_adapter.reshape(1, rows), inputs, cotangent, base_weight,
        jnp.swapaxes(down_a, 1, 2), up_b,
    )


def solution(mesh):
    in_specs = (
        P("dp", "tensor"),
        P("dp", "tensor"),
        P("tensor", None),
        P("dp", "tensor", None),
        P("dp", None, "tensor"),
        P("dp"),
        P("dp"),
        P(),
    )
    out_specs = (P("dp", "tensor"), P("dp", None, "tensor"))
    return jax.shard_map(
        functools.partial(on_device, mesh.shape["dp"], mesh.shape["tensor"]),
        mesh=mesh, in_specs=in_specs, out_specs=out_specs, check_vma=False,
    )
```

time: 41.9 us -> 35.1 us (0.84)
  local copies, waits for them, and re-layouts: 9.27 us -> 3.08 us
    unnamed x18 -> x4, local copies, waits for them, and re-layouts: 9.27 us -> 3.08 us
where the time goes in v2:
time: 35.1 us; the launch traced here: 35 us
  Pallas kernels  31.2 us (89%)
  local copies, waits for them, and re-layouts  3.08 us (9%)
  between operations  0.65 us (2%)
    pallas_call x1, Pallas kernels, on_device(): pl.pallas_call(functools.partial(kernel, ndp, nten), out_shape=(jax.Shape...  31.2 us
    unnamed x4, local copies, waits for them, and re-layouts  3.08 us

profile of v2, /device:TPU:0, one launch (start us, length us, event | category | flops | bytes accessed | tf_op | source)
XLA Modules:
  0.0 35.0 jit_solution(17747875525377886790)
XLA Ops:
  0.6 31.2 %shard_map.95 = (bf16[512,1280]{1,0:T(8,128)(2,1)}, f32[2,16,256]{2,1,0:T(8,128)}) custom-call(s32[16]{0:T(128)} %owner_ref.1, s32[4]{0:T(128)} %block_ref.1, s32[1,512]{1,0:T(1,128)} %bitcast.3, bf16[512,1280]{1,0:T(8,128)(2,1)} %x_ref.1, bf16[512,256]{1,0:T(8,128)(2,1)} %g_ref.1, bf16[1280,1024]{1,0:T(8,128)(2,1)} %w_ref.1, bf16[2,16,1280]{2,1,0:T(8,128)(2,1)} %bitcast.2, ...), custom_call_target="tpu_custom_call" | custom-call | flops 1384120320 | bytes 5505024 | tf_op jit(solution)/shard_map/pallas_call | solution.py:365
  31.9 0.0 copy-start
  31.9 2.5 %copy.12 = bf16[512,1280]{1,0:T(8,128)(2,1)} copy(bf16[512,1280]{1,0:T(8,128)(2,1)} %get-tuple-element.4) | data formatting | bytes 2621440
  34.4 0.0 copy-done
  34.4 0.6 %copy.13 = f32[2,16,256]{2,1,0:T(8,128)} copy(f32[2,16,256]{2,1,0:T(8,128)S(1)} %copy-done) | data formatting | bytes 65536
Async XLA Ops:
  31.9 2.5 %copy-start = (f32[2,16,256]{2,1,0:T(8,128)S(1)}, f32[2,16,256]{2,1,0:T(8,128)}, u32[]{:S(2)}) copy-start(f32[2,16,256]{2,1,0:T(8,128)} %get-tuple-element.5) | copy-start | bytes 98308

commit v3 on v2

--- a/solution.py
+++ b/solution.py
@@ -25,7 +25,7 @@
     ndp, nten, owner_ref, block_ref, tok_ref, x_ref, g_ref, w_ref, a_ref, u_ref,
     out_ref, grad_ref,
     owner, block, tok, xv, wv, gall, gm, acc, aall, uall, part, outv, gsend, grecv,
-    local_sem, w_sem, out_sem, a_send, a_recv, g_send, g_fwd, g_recv,
+    local_sem, w_sem, out_sem, a_send, a_recv, u_send, u_recv, g_send, g_fwd, g_recv,
     p_send, p_recv, r_send, r_recv,
 ):
     nblk = block_ref.shape[0]
@@ -82,23 +82,41 @@
         cp.start()
     pl.semaphore_wait(barrier, ndp + nten - 2)
 
-    def hop(src, way, first):
-        at = pl.ds(src * own, own)
+    def hop(src, k, way, first):
+        slot = src * own + k
         if way == 2:
             to = inner * z + 1 - y
         else:
             to = inner * (z + 1 - 2 * way) + y
-        return [
-            pltpu.make_async_remote_copy(
-                src_ref=(ref if first else full.at[at]),
-                dst_ref=full.at[at],
-                send_sem=a_send.at[i, way, src],
-                recv_sem=a_recv.at[i, src],
-                device_id=(to, t),
-                device_id_type=MESH,
-            )
-            for i, (ref, full) in enumerate(((a_ref, aall), (u_ref, uall)))
-        ]
+        return pltpu.make_async_remote_copy(
+            src_ref=(a_ref.at[k] if first else aall.at[slot]),
+            dst_ref=aall.at[slot],
+            send_sem=a_send.at[way, slot],
+            recv_sem=a_recv.at[slot],
+            device_id=(to, t),
+            device_id_type=MESH,
+        )
+
+    def to_peer(j):
+        return pltpu.make_async_remote_copy(
+            src_ref=u_ref,
+            dst_ref=uall.at[mine],
+            send_sem=u_send.at[j],
+            recv_sem=u_recv.at[j],
+            device_id=(lax.rem(me + j, ndp), t),
+            device_id_type=MESH,
+        )
+
+    def from_peer(j):
+        at = pl.ds(lax.rem(me + ndp - j, ndp) * own, own)
+        pltpu.make_async_remote_copy(
+            src_ref=u_ref,
+            dst_ref=uall.at[at],
+            send_sem=u_send.at[j],
+            recv_sem=u_recv.at[j],
+            device_id=(lax.rem(me + j, ndp), t),
+            device_id_type=MESH,
+        ).wait_recv()
 
     def for_ways(fn, ways):
         for way in ways:
@@ -109,27 +127,22 @@
                 ok = z + 1 < outer if way == 0 else z > 0
                 pl.when(ok)(functools.partial(fn, way))
 
-    def start_hops(src, ways, first=False):
-        def go(way):
-            for cp in hop(src, way, first):
-                cp.start()
-
-        for_ways(go, ways)
-
-    def wait_hops(src, ways, first=False):
-        def go(way):
-            for cp in hop(src, way, first):
-                cp.wait_send()
-
-        for_ways(go, ways)
-
-    def got_hop(src):
-        for cp in hop(src, 0, False):
-            cp.wait_recv()
-
-    def line(k, fn):
-        pl.when(z - k >= 0)(lambda: fn(inner * (z - k) + y, (0, 2)))
-        pl.when(z + k < outer)(lambda: fn(inner * (z + k) + y, (1, 2)))
+    def start_hops(src, k, ways, first=False):
+        for_ways(lambda way: hop(src, k, way, first).start(), ways)
+
+    def wait_hops(src, k, ways, first=False):
+        for_ways(lambda way: hop(src, k, way, first).wait_send(), ways)
+
+    def got_hop(src, k):
+        hop(src, k, 0, False).wait_recv()
+
+    def line(d, k, fn):
+        pl.when(z - d >= 0)(lambda: fn(inner * (z - d) + y, k, (0, 2)))
+        pl.when(z + d < outer)(lambda: fn(inner * (z + d) + y, k, (1, 2)))
+
+    def lines(d, fn):
+        for k in range(own):
+            line(d, k, fn)
 
     def span_of(i):
         return pl.ds(i * brows, brows)
@@ -165,7 +178,8 @@
             device_id_type=MESH,
         ).wait_recv()
 
-    start_hops(me, (0, 1, 2), True)
+    for k in range(own):
+        start_hops(me, k, (0, 1, 2), True)
     for i in range(nblk):
         for j in range(1, nx):
             g_own(2 * j, i).start()
@@ -205,9 +219,9 @@
     mask_piece(0)
     multiply(0)
 
-    def pass_on(src, ways):
-        got_hop(src)
-        start_hops(src, ways)
+    def pass_on(src, k, ways):
+        got_hop(src, k)
+        start_hops(src, k, ways)
 
     def pass_g(i):
         for j in range(1, nx):
@@ -223,16 +237,17 @@
     if outer <= 4:
         for k in range(1, max(outer, nblk + 1)):
             if k < outer:
-                line(k, pass_on)
+                lines(k, pass_on)
             if k == 1:
                 twin_piece()
             if k <= nblk:
                 pass_g(k - 1)
     else:
-        loop(1, outer, lambda k: line(k, pass_on))
+        loop(1, outer, lambda d: lines(d, pass_on))
         twin_piece()
         for i in range(nblk):
             pass_g(i)
+    loop(1, ndp, lambda j: to_peer(j).start())
     for j in range(1, nx):
         mask_piece(2 * j)
 
@@ -240,7 +255,8 @@
         cp.wait()
     slots = [owner[block[b]] for b in range(nblk)]
     if inner == 2:
-        loop(0, outer, lambda k: got_hop(inner * k + 1 - y))
+        for k in range(own):
+            loop(0, outer, lambda d: got_hop(inner * d + 1 - y, k))
 
     def to_ten(which, rel):
         return pltpu.make_async_remote_copy(
@@ -257,6 +273,8 @@
         ).wait_recv()
 
     for which, (pieces, act) in enumerate(((aall, xv), (uall, gall.at[0]))):
+        if which == 1:
+            loop(1, ndp, from_peer)
         for b in range(nblk):
             span = slice(b * brows, (b + 1) * brows)
             part[which, 0, :, span] = lax.dot_general(
@@ -327,8 +345,10 @@
         cp.start()
         outs.append(cp)
 
-    wait_hops(me, (0, 1, 2), True)
-    loop(1, outer, lambda k: line(k, wait_hops))
+    for k in range(own):
+        wait_hops(me, k, (0, 1, 2), True)
+    loop(1, outer, lambda d: lines(d, wait_hops))
+    loop(1, ndp, lambda j: to_peer(j).wait_send())
     for i in range(nblk):
         for j in range(1, nx):
             g_own(2 * j, i).wait_send()
@@ -345,6 +365,19 @@
     loop(1, ndp, gather_grad)
     loop(1, ndp, lambda j: to_owner(j).wait_send())
     for cp in outs:
+        cp.wait()
+
+
+def hand_over(out_ref, grad_ref, out_to, grad_to, sem):
+    parts = sem.shape[0] - 1
+    rows = out_ref.shape[0] // parts
+    copies = [pltpu.make_async_copy(grad_ref, grad_to, sem.at[parts])]
+    for i in range(parts):
+        at = pl.ds(i * rows, rows)
+        copies.append(pltpu.make_async_copy(out_ref.at[at], out_to.at[at], sem.at[i]))
+    for cp in copies:
+        cp.start()
+    for cp in copies:
         cp.wait()
 
 
@@ -362,7 +395,7 @@
     bf16, f32 = jnp.bfloat16, jnp.float32
     hbm = pl.BlockSpec(memory_space=pltpu.HBM)
     dma = pltpu.SemaphoreType.DMA
-    return pl.pallas_call(
+    results = pl.pallas_call(
         functools.partial(kernel, ndp, nten),
         out_shape=(
             jax.ShapeDtypeStruct((rows, dpiece), bf16),
@@ -388,8 +421,10 @@
             dma((7,)),
             dma((nten,)),
             dma((dpiece // tile,)),
-            dma((2, 3, ndp)),
-            dma((2, ndp)),
+            dma((3, slots)),
+            dma((slots,)),
+            dma((ndp,)),
+            dma((ndp,)),
             dma((nten, nblk)),
             dma((nx, nblk)),
             dma((nten, nblk)),
@@ -410,6 +445,17 @@
         owner_map, block_adapter, token_adapter.reshape(1, rows), inputs, cotangent, base_weight,
         jnp.swapaxes(down_a, 1, 2), up_b,
     )
+    return pl.pallas_call(
+        hand_over,
+        out_shape=tuple(jax.ShapeDtypeStruct(r.shape, r.dtype) for r in results),
+        in_specs=[hbm] * 2,
+        out_specs=(hbm, hbm),
+        scratch_shapes=[dma((nblk + 1,))],
+        cost_estimate=pl.CostEstimate(
+            flops=0, bytes_accessed=4 * rows * dpiece, transcendentals=0
+        ),
+        compiler_params=pltpu.CompilerParams(vmem_limit_bytes=64 * 2**20 - 2**18),
+    )(*results)
 
 
 def solution(mesh):

time: 35.1 us -> 72 us (2.05)
  Pallas kernels: 31.2 us -> 71.2 us
  local copies, waits for them, and re-layouts: 3.08 us -> 0 us
    pallas_call x0 -> x1, Pallas kernels: none -> 41.8 us  [on_device(): pl.pallas_call(hand_over, out_shape=tuple((jax.ShapeDtypeStruct(r.shape,...]
    unnamed x4 -> x0, local copies, waits for them, and re-layouts: 3.08 us -> none
    pallas_call x1, Pallas kernels: 31.2 us -> 29.4 us  [on_device(): pl.pallas_call(functools.partial(kernel, ndp, nten), out_shape=(jax.Shape...]
where the time goes in v3:
time: 72 us; the launch traced here: 71.9 us
  Pallas kernels  71.2 us (99%)
    pallas_call x1, Pallas kernels, on_device(): pl.pallas_call(hand_over, out_shape=tuple((jax.ShapeDtypeStruct(r.shape,...  41.8 us
    pallas_call x1, Pallas kernels, on_device(): pl.pallas_call(functools.partial(kernel, ndp, nten), out_shape=(jax.Shape...  29.4 us

profile of v3, /device:TPU:0, one launch (start us, length us, event | category | flops | bytes accessed | tf_op | source)
XLA Modules:
  0.0 71.9 jit_solution(14351078963071335836)
XLA Ops:
  0.6 29.4 %shard_map.95 = (bf16[512,1280]{1,0:T(8,128)(2,1)}, f32[2,16,256]{2,1,0:T(8,128)}) custom-call(s32[16]{0:T(128)} %owner_ref.1, s32[4]{0:T(128)} %block_ref.1, s32[1,512]{1,0:T(1,128)} %bitcast.3, bf16[512,1280]{1,0:T(8,128)(2,1)} %x_ref.1, bf16[512,256]{1,0:T(8,128)(2,1)} %g_ref.1, bf16[1280,1024]{1,0:T(8,128)(2,1)} %w_ref.1, bf16[2,16,1280]{2,1,0:T(8,128)(2,1)} %bitcast.2, ...), custom_call_target="tpu_custom_call" | custom-call | flops 1384120320 | bytes 5505024 | tf_op jit(solution)/shard_map/pallas_call | solution.py:398
  30.0 41.8 %shard_map.96 = (bf16[512,1280]{1,0:T(8,128)(2,1)}, f32[2,16,256]{2,1,0:T(8,128)}) custom-call(bf16[512,1280]{1,0:T(8,128)(2,1)} %get-tuple-element.4.out_ref, f32[2,16,256]{2,1,0:T(8,128)} %get-tuple-element.5.grad_ref), custom_call_target="tpu_custom_call" | custom-call | bytes 2621440 | tf_op jit(solution)/shard_map/pallas_call | solution.py:448

commit v4 on v3

--- a/solution.py
+++ b/solution.py
@@ -217,7 +217,6 @@
 
     local[1].wait()
     mask_piece(0)
-    multiply(0)
 
     def pass_on(src, k, ways):
         got_hop(src, k)
@@ -238,18 +237,22 @@
         for k in range(1, max(outer, nblk + 1)):
             if k < outer:
                 lines(k, pass_on)
-            if k == 1:
-                twin_piece()
             if k <= nblk:
                 pass_g(k - 1)
+            if k == 1:
+                multiply(0)
+            if k == 2:
+                twin_piece()
     else:
         loop(1, outer, lambda d: lines(d, pass_on))
+        multiply(0)
         twin_piece()
         for i in range(nblk):
             pass_g(i)
     loop(1, ndp, lambda j: to_peer(j).start())
     for j in range(1, nx):
         mask_piece(2 * j)
+        multiply(2 * j)
 
     for cp in local[2:]:
         cp.wait()
@@ -284,7 +287,10 @@
             to_ten(which, rel).start()
 
     for j in range(1, nx):
-        multiply(2 * j)
+        for i in range(nblk):
+            g_wait(2 * j + 1, i)
+        mask_piece(2 * j + 1)
+        multiply(2 * j + 1)
 
     def summed(which):
         total = part[which, 0]
@@ -325,11 +331,6 @@
     for s in range(own):
         grad_ref[s] = share(me, s)
 
-    for j in range(1, nx):
-        for i in range(nblk):
-            g_wait(2 * j + 1, i)
-        mask_piece(2 * j + 1)
-        multiply(2 * j + 1)
     hidden = summed(1) * jnp.bfloat16(adapter_scale_factor)
     outs = []
     for n in range(tiles):
@@ -368,16 +369,21 @@
         cp.wait()
 
 
-def hand_over(out_ref, grad_ref, out_to, grad_to, sem):
-    parts = sem.shape[0] - 1
+def hand_over(out_ref, grad_ref, out_to, grad_to, out_held, grad_held, sem_in, sem_out):
+    parts = sem_in.shape[0] - 1
     rows = out_ref.shape[0] // parts
-    copies = [pltpu.make_async_copy(grad_ref, grad_to, sem.at[parts])]
+    ways = [(grad_ref, grad_held, grad_to)]
     for i in range(parts):
         at = pl.ds(i * rows, rows)
-        copies.append(pltpu.make_async_copy(out_ref.at[at], out_to.at[at], sem.at[i]))
-    for cp in copies:
+        ways.append((out_ref.at[at], out_held.at[at], out_to.at[at]))
+    ins = [pltpu.make_async_copy(a, b, sem_in.at[i]) for i, (a, b, _) in enumerate(ways)]
+    outs = [pltpu.make_async_copy(b, c, sem_out.at[i]) for i, (_, b, c) in enumerate(ways)]
+    for cp in ins:
         cp.start()
-    for cp in copies:
+    for cp, then in zip(ins, outs):
+        cp.wait()
+        then.start()
+    for cp in outs:
         cp.wait()
 
 
@@ -450,7 +456,12 @@
         out_shape=tuple(jax.ShapeDtypeStruct(r.shape, r.dtype) for r in results),
         in_specs=[hbm] * 2,
         out_specs=(hbm, hbm),
-        scratch_shapes=[dma((nblk + 1,))],
+        scratch_shapes=[
+            pltpu.VMEM((rows, dpiece), bf16),
+            pltpu.VMEM((own, rank, kpiece), f32),
+            dma((nblk + 1,)),
+            dma((nblk + 1,)),
+        ],
         cost_estimate=pl.CostEstimate(
             flops=0, bytes_accessed=4 * rows * dpiece, transcendentals=0
         ),

time: 72 us -> 32.8 us (0.46)
  Pallas kernels: 71.2 us -> 32 us
    pallas_call x1, Pallas kernels: 41.8 us -> 2.13 us  [on_device(): pl.pallas_call(hand_over, out_shape=tuple((jax.ShapeDtypeStruct(r.shape,...]
where the time goes in v4:
time: 32.8 us; the launch traced here: 32.7 us
  Pallas kernels  32 us (98%)
  between operations  0.64 us (2%)
    pallas_call x1, Pallas kernels, on_device(): pl.pallas_call(functools.partial(kernel, ndp, nten), out_shape=(jax.Shape...  29.9 us
    pallas_call x1, Pallas kernels, on_device(): pl.pallas_call(hand_over, out_shape=tuple((jax.ShapeDtypeStruct(r.shape,...  2.13 us

profile of v4, /device:TPU:0, one launch (start us, length us, event | category | flops | bytes accessed | tf_op | source)
XLA Modules:
  0.0 32.7 jit_solution(5288528188874852681)
XLA Ops:
  0.6 29.9 %shard_map.95 = (bf16[512,1280]{1,0:T(8,128)(2,1)}, f32[2,16,256]{2,1,0:T(8,128)}) custom-call(s32[16]{0:T(128)} %owner_ref.1, s32[4]{0:T(128)} %block_ref.1, s32[1,512]{1,0:T(1,128)} %bitcast.3, bf16[512,1280]{1,0:T(8,128)(2,1)} %x_ref.1, bf16[512,256]{1,0:T(8,128)(2,1)} %g_ref.1, bf16[1280,1024]{1,0:T(8,128)(2,1)} %w_ref.1, bf16[2,16,1280]{2,1,0:T(8,128)(2,1)} %bitcast.2, ...), custom_call_target="tpu_custom_call" | custom-call | flops 1384120320 | bytes 5505024 | tf_op jit(solution)/shard_map/pallas_call | solution.py:404
  30.5 2.1 %shard_map.96 = (bf16[512,1280]{1,0:T(8,128)(2,1)}, f32[2,16,256]{2,1,0:T(8,128)}) custom-call(bf16[512,1280]{1,0:T(8,128)(2,1)} %get-tuple-element.4.out_ref, f32[2,16,256]{2,1,0:T(8,128)} %get-tuple-element.5.grad_ref), custom_call_target="tpu_custom_call" | custom-call | bytes 2621440 | tf_op jit(solution)/shard_map/pallas_call | solution.py:454

commit v5 on v4

--- a/solution.py
+++ b/solution.py
@@ -74,7 +74,7 @@
     weights = [
         pltpu.make_async_copy(
             w_ref.at[:, pl.ds(pl.multiple_of(ten_of(rel) * kpiece, kpiece), kpiece)],
-            wv.at[rel], w_sem.at[rel],
+            wv.at[:, pl.ds(rel * kpiece, kpiece)], w_sem.at[rel],
         )
         for rel in range(nten)
     ]
@@ -197,20 +197,25 @@
 
     def mask_piece(rel):
         for b in range(nblk):
-            gm[rel, span_of(b), :] = gall[rel, span_of(b), :] * tall[b]
-
-    def multiply(rel):
-        weights[rel].wait()
+            gm[span_of(b), rel * kpiece:(rel + 1) * kpiece] = gall[rel, span_of(b), :] * tall[b]
+
+    near = 2 * kpiece
+
+    def product(cols, lo, hi):
+        return lax.dot_general(
+            gm[:, lo:hi], wv[cols, lo:hi], LAST, preferred_element_type=jnp.float32
+        )
+
+    def near_product():
+        for i in range(nblk):
+            g_wait(1, i)
+        mask_piece(1)
+        for cp in weights[:2]:
+            cp.wait()
 
         def one(n, carry):
             cols = pl.ds(pl.multiple_of(n * tile, tile), tile)
-            prod = lax.dot_general(
-                gm[rel], wv[rel, cols, :], LAST, preferred_element_type=jnp.float32
-            )
-            if rel == 0:
-                acc[n] = prod
-            else:
-                acc[n] += prod
+            acc[n] = product(cols, 0, near)
             return carry
 
         lax.fori_loop(0, tiles, one, 0)
@@ -227,32 +232,15 @@
             g_wait(2 * j, i)
             g_pass(j, i).start()
 
-    def twin_piece():
-        for i in range(nblk):
-            g_wait(1, i)
-        mask_piece(1)
-        multiply(1)
-
     if outer <= 4:
-        for k in range(1, max(outer, nblk + 1)):
-            if k < outer:
-                lines(k, pass_on)
-            if k <= nblk:
-                pass_g(k - 1)
-            if k == 1:
-                multiply(0)
-            if k == 2:
-                twin_piece()
+        for d in range(1, outer):
+            lines(d, pass_on)
+            if d == 1:
+                near_product()
     else:
+        near_product()
         loop(1, outer, lambda d: lines(d, pass_on))
-        multiply(0)
-        twin_piece()
-        for i in range(nblk):
-            pass_g(i)
     loop(1, ndp, lambda j: to_peer(j).start())
-    for j in range(1, nx):
-        mask_piece(2 * j)
-        multiply(2 * j)
 
     for cp in local[2:]:
         cp.wait()
@@ -286,27 +274,26 @@
         for rel in range(nten - 1, 0, -1):
             to_ten(which, rel).start()
 
+    for i in range(nblk):
+        pass_g(i)
     for j in range(1, nx):
-        for i in range(nblk):
-            g_wait(2 * j + 1, i)
-        mask_piece(2 * j + 1)
-        multiply(2 * j + 1)
+        mask_piece(2 * j)
 
     def summed(which):
         total = part[which, 0]
         for rel in range(1, nten):
             from_ten(which, rel)
             total = total + part[which, rel]
-        return (total * live).astype(jnp.bfloat16)
-
-    lowrank = summed(0)
+        return total * live
+
+    lowrank = summed(0).astype(jnp.bfloat16)
 
     terms = []
     for b in range(nblk):
         span = slice(b * brows, (b + 1) * brows)
         terms.append(
             adapter_scale_factor
-            * jnp.dot(lowrank[:, span], gm[0, span, :], preferred_element_type=jnp.float32)
+            * jnp.dot(lowrank[:, span], gm[span, :kpiece], preferred_element_type=jnp.float32)
         )
 
     def share(dev, s):
@@ -331,20 +318,35 @@
     for s in range(own):
         grad_ref[s] = share(me, s)
 
-    hidden = summed(1) * jnp.bfloat16(adapter_scale_factor)
-    outs = []
-    for n in range(tiles):
-        cols = slice(n * tile, (n + 1) * tile)
+    for j in range(1, nx):
+        for i in range(nblk):
+            g_wait(2 * j + 1, i)
+        mask_piece(2 * j + 1)
+    for cp in weights[2:]:
+        cp.wait()
+    hidden = summed(1)
+    scaled = [
+        hidden[:, b * brows:(b + 1) * brows].T.astype(jnp.bfloat16)
+        * jnp.bfloat16(adapter_scale_factor)
+        for b in range(nblk)
+    ]
+    kout = wv.shape[1]
+
+    def to_out(n):
+        cols = pl.ds(pl.multiple_of(n * tile, tile), tile)
+        return pltpu.make_async_copy(outv.at[n], out_ref.at[:, cols], out_sem.at[n])
+
+    def last(n, carry):
+        cols = pl.ds(pl.multiple_of(n * tile, tile), tile)
+        base = acc[n] + product(cols, near, kout) if nx > 1 else acc[n]
         for b in range(nblk):
             span = slice(b * brows, (b + 1) * brows)
-            low = lax.dot_general(
-                hidden[:, span], aall[slots[b], :, cols], FIRST,
-                preferred_element_type=jnp.float32,
-            )
-            outv[n, span, :] = (acc[n, span, :] + low).astype(jnp.bfloat16)
-        cp = pltpu.make_async_copy(outv.at[n], out_ref.at[:, cols], out_sem.at[n])
-        cp.start()
-        outs.append(cp)
+            low = jnp.dot(scaled[b], aall[slots[b], :, cols], preferred_element_type=jnp.float32)
+            outv[n, span, :] = (base[span] + low).astype(jnp.bfloat16)
+        to_out(n).start()
+        return carry
+
+    lax.fori_loop(0, tiles, last, 0)
 
     for k in range(own):
         wait_hops(me, k, (0, 1, 2), True)
@@ -365,8 +367,8 @@
 
     loop(1, ndp, gather_grad)
     loop(1, ndp, lambda j: to_owner(j).wait_send())
-    for cp in outs:
-        cp.wait()
+    for n in range(tiles):
+        to_out(n).wait()
 
 
 def hand_over(out_ref, grad_ref, out_to, grad_to, out_held, grad_held, sem_in, sem_out):
@@ -414,9 +416,9 @@
             pltpu.SMEM((nblk,), jnp.int32),
             pltpu.VMEM((1, rows), jnp.int32),
             pltpu.VMEM((rows, dpiece), bf16),
-            pltpu.VMEM((nten, dpiece, kpiece), bf16),
+            pltpu.VMEM((dpiece, kout), bf16),
             pltpu.VMEM((nten, rows, kpiece), bf16),
-            pltpu.VMEM((nten, rows, kpiece), bf16),
+            pltpu.VMEM((rows, kout), bf16),
             pltpu.VMEM((dpiece // tile, rows, tile), f32),
             pltpu.VMEM((slots, rank, dpiece), bf16),
             pltpu.VMEM((slots, rank, kpiece), bf16),

time: 32.8 us -> 32.3 us (0.985)
  Pallas kernels: 32 us -> 31.5 us
    pallas_call x1, Pallas kernels: 29.9 us -> 29.4 us  [on_device(): pl.pallas_call(functools.partial(kernel, ndp, nten), out_shape=(jax.Shape...]
where the time goes in v5:
time: 32.3 us; the launch traced here: 32.1 us
  Pallas kernels  31.5 us (98%)
  between operations  0.64 us (2%)
    pallas_call x1, Pallas kernels, on_device(): pl.pallas_call(functools.partial(kernel, ndp, nten), out_shape=(jax.Shape...  29.4 us
    pallas_call x1, Pallas kernels, on_device(): pl.pallas_call(hand_over, out_shape=tuple((jax.ShapeDtypeStruct(r.shape,...  2.13 us

profile of v5, /device:TPU:0, one launch (start us, length us, event | category | flops | bytes accessed | tf_op | source)
XLA Modules:
  0.0 32.1 jit_solution(3149889662288196537)
XLA Ops:
  0.6 29.4 %shard_map.95 = (bf16[512,1280]{1,0:T(8,128)(2,1)}, f32[2,16,256]{2,1,0:T(8,128)}) custom-call(s32[16]{0:T(128)} %owner_ref.1, s32[4]{0:T(128)} %block_ref.1, s32[1,512]{1,0:T(1,128)} %bitcast.3, bf16[512,1280]{1,0:T(8,128)(2,1)} %x_ref.1, bf16[512,256]{1,0:T(8,128)(2,1)} %g_ref.1, bf16[1280,1024]{1,0:T(8,128)(2,1)} %w_ref.1, bf16[2,16,1280]{2,1,0:T(8,128)(2,1)} %bitcast.2, ...), custom_call_target="tpu_custom_call" | custom-call | flops 1384120320 | bytes 5505024 | tf_op jit(solution)/shard_map/pallas_call | solution.py:406
  30.0 2.1 %shard_map.96 = (bf16[512,1280]{1,0:T(8,128)(2,1)}, f32[2,16,256]{2,1,0:T(8,128)}) custom-call(bf16[512,1280]{1,0:T(8,128)(2,1)} %get-tuple-element.4.out_ref, f32[2,16,256]{2,1,0:T(8,128)} %get-tuple-element.5.grad_ref), custom_call_target="tpu_custom_call" | custom-call | bytes 2621440 | tf_op jit(solution)/shard_map/pallas_call | solution.py:456

commit v6 on v5

--- a/solution.py
+++ b/solution.py
@@ -240,8 +240,6 @@
     else:
         near_product()
         loop(1, outer, lambda d: lines(d, pass_on))
-    loop(1, ndp, lambda j: to_peer(j).start())
-
     for cp in local[2:]:
         cp.wait()
     slots = [owner[block[b]] for b in range(nblk)]
@@ -263,9 +261,7 @@
             device_id=(me, ten_of(rel)), device_id_type=MESH,
         ).wait_recv()
 
-    for which, (pieces, act) in enumerate(((aall, xv), (uall, gall.at[0]))):
-        if which == 1:
-            loop(1, ndp, from_peer)
+    def send_partial(which, pieces, act):
         for b in range(nblk):
             span = slice(b * brows, (b + 1) * brows)
             part[which, 0, :, span] = lax.dot_general(
@@ -274,6 +270,9 @@
         for rel in range(nten - 1, 0, -1):
             to_ten(which, rel).start()
 
+    send_partial(0, aall, xv)
+    loop(1, ndp, lambda j: to_peer(j).start())
+
     for i in range(nblk):
         pass_g(i)
     for j in range(1, nx):
@@ -318,19 +317,29 @@
     for s in range(own):
         grad_ref[s] = share(me, s)
 
+    loop(1, ndp, from_peer)
+    send_partial(1, uall, gall.at[0])
     for j in range(1, nx):
         for i in range(nblk):
             g_wait(2 * j + 1, i)
         mask_piece(2 * j + 1)
     for cp in weights[2:]:
         cp.wait()
+    kout = wv.shape[1]
+
+    def far_product(n, carry):
+        cols = pl.ds(pl.multiple_of(n * tile, tile), tile)
+        acc[n] += product(cols, near, kout)
+        return carry
+
+    if nx > 1:
+        lax.fori_loop(0, tiles, far_product, 0)
     hidden = summed(1)
     scaled = [
         hidden[:, b * brows:(b + 1) * brows].T.astype(jnp.bfloat16)
         * jnp.bfloat16(adapter_scale_factor)
         for b in range(nblk)
     ]
-    kout = wv.shape[1]
 
     def to_out(n):
         cols = pl.ds(pl.multiple_of(n * tile, tile), tile)
@@ -338,11 +347,10 @@
 
     def last(n, carry):
         cols = pl.ds(pl.multiple_of(n * tile, tile), tile)
-        base = acc[n] + product(cols, near, kout) if nx > 1 else acc[n]
         for b in range(nblk):
             span = slice(b * brows, (b + 1) * brows)
             low = jnp.dot(scaled[b], aall[slots[b], :, cols], preferred_element_type=jnp.float32)
-            outv[n, span, :] = (base[span] + low).astype(jnp.bfloat16)
+            outv[n, span, :] = (acc[n, span, :] + low).astype(jnp.bfloat16)
         to_out(n).start()
         return carry
 

time: 32.3 us -> 34.4 us (1.065)
  Pallas kernels: 31.5 us -> 33.6 us
    pallas_call x1, Pallas kernels: 29.4 us -> 31.4 us  [on_device(): pl.pallas_call(functools.partial(kernel, ndp, nten), out_shape=(jax.Shape...]
where the time goes in v6:
time: 34.4 us; the launch traced here: 34.2 us
  Pallas kernels  33.6 us (98%)
  between operations  0.64 us (2%)
    pallas_call x1, Pallas kernels, on_device(): pl.pallas_call(functools.partial(kernel, ndp, nten), out_shape=(jax.Shape...  31.4 us
    pallas_call x1, Pallas kernels, on_device(): pl.pallas_call(hand_over, out_shape=tuple((jax.ShapeDtypeStruct(r.shape,...  2.13 us

profile of v6, /device:TPU:0, one launch (start us, length us, event | category | flops | bytes accessed | tf_op | source)
XLA Modules:
  0.0 34.2 jit_solution(6327976615622114707)
XLA Ops:
  0.6 31.4 %shard_map.95 = (bf16[512,1280]{1,0:T(8,128)(2,1)}, f32[2,16,256]{2,1,0:T(8,128)}) custom-call(s32[16]{0:T(128)} %owner_ref.1, s32[4]{0:T(128)} %block_ref.1, s32[1,512]{1,0:T(1,128)} %bitcast.3, bf16[512,1280]{1,0:T(8,128)(2,1)} %x_ref.1, bf16[512,256]{1,0:T(8,128)(2,1)} %g_ref.1, bf16[1280,1024]{1,0:T(8,128)(2,1)} %w_ref.1, bf16[2,16,1280]{2,1,0:T(8,128)(2,1)} %bitcast.2, ...), custom_call_target="tpu_custom_call" | custom-call | flops 1384120320 | bytes 5505024 | tf_op jit(solution)/shard_map/pallas_call | solution.py:414
  32.1 2.1 %shard_map.96 = (bf16[512,1280]{1,0:T(8,128)(2,1)}, f32[2,16,256]{2,1,0:T(8,128)}) custom-call(bf16[512,1280]{1,0:T(8,128)(2,1)} %get-tuple-element.4.out_ref, f32[2,16,256]{2,1,0:T(8,128)} %get-tuple-element.5.grad_ref), custom_call_target="tpu_custom_call" | custom-call | bytes 2621440 | tf_op jit(solution)/shard_map/pallas_call | solution.py:464

commit v7 on v5

--- a/solution.py
+++ b/solution.py
@@ -179,7 +179,10 @@
         ).wait_recv()
 
     for k in range(own):
-        start_hops(me, k, (0, 1, 2), True)
+        start_hops(me, k, (0, 1), True)
+    loop(1, ndp, lambda j: to_peer(j).start())
+    for k in range(own):
+        start_hops(me, k, (2,), True)
     for i in range(nblk):
         for j in range(1, nx):
             g_own(2 * j, i).start()
@@ -232,7 +235,35 @@
             g_wait(2 * j, i)
             g_pass(j, i).start()
 
+    def to_ten(which, rel):
+        return pltpu.make_async_remote_copy(
+            src_ref=part.at[which, 0], dst_ref=part.at[which, place_there(rel)],
+            send_sem=p_send.at[which, rel], recv_sem=p_recv.at[which, place_there(rel)],
+            device_id=(me, ten_of(rel)), device_id_type=MESH,
+        )
+
+    def from_ten(which, rel):
+        pltpu.make_async_remote_copy(
+            src_ref=part.at[which, 0], dst_ref=part.at[which, rel],
+            send_sem=p_send.at[which, rel], recv_sem=p_recv.at[which, rel],
+            device_id=(me, ten_of(rel)), device_id_type=MESH,
+        ).wait_recv()
+
+    def send_partial(which, pieces, act):
+        for b in range(nblk):
+            span = slice(b * brows, (b + 1) * brows)
+            part[which, 0, :, span] = lax.dot_general(
+                pieces[slots[b]], act[span, :], LAST, preferred_element_type=jnp.float32
+            )
+        for rel in range(nten - 1, 0, -1):
+            to_ten(which, rel).start()
+
+    for cp in local[2:]:
+        cp.wait()
+    slots = [owner[block[b]] for b in range(nblk)]
     if outer <= 4:
+        if outer < 2:
+            near_product()
         for d in range(1, outer):
             lines(d, pass_on)
             if d == 1:
@@ -240,39 +271,13 @@
     else:
         near_product()
         loop(1, outer, lambda d: lines(d, pass_on))
-    loop(1, ndp, lambda j: to_peer(j).start())
-
-    for cp in local[2:]:
-        cp.wait()
-    slots = [owner[block[b]] for b in range(nblk)]
+    loop(1, ndp, from_peer)
+    send_partial(1, uall, gall.at[0])
     if inner == 2:
         for k in range(own):
             loop(0, outer, lambda d: got_hop(inner * d + 1 - y, k))
 
-    def to_ten(which, rel):
-        return pltpu.make_async_remote_copy(
-            src_ref=part.at[which, 0], dst_ref=part.at[which, place_there(rel)],
-            send_sem=p_send.at[which, rel], recv_sem=p_recv.at[which, place_there(rel)],
-            device_id=(me, ten_of(rel)), device_id_type=MESH,
-        )
-
-    def from_ten(which, rel):
-        pltpu.make_async_remote_copy(
-            src_ref=part.at[which, 0], dst_ref=part.at[which, rel],
-            send_sem=p_send.at[which, rel], recv_sem=p_recv.at[which, rel],
-            device_id=(me, ten_of(rel)), device_id_type=MESH,
-        ).wait_recv()
-
-    for which, (pieces, act) in enumerate(((aall, xv), (uall, gall.at[0]))):
-        if which == 1:
-            loop(1, ndp, from_peer)
-        for b in range(nblk):
-            span = slice(b * brows, (b + 1) * brows)
-            part[which, 0, :, span] = lax.dot_general(
-                pieces[slots[b]], act[span, :], LAST, preferred_element_type=jnp.float32
-            )
-        for rel in range(nten - 1, 0, -1):
-            to_ten(which, rel).start()
+    send_partial(0, aall, xv)
 
     for i in range(nblk):
         pass_g(i)

time: 32.3 us -> 33.2 us (1.028)
  Pallas kernels: 31.5 us -> 32.4 us
    pallas_call x1, Pallas kernels: 29.4 us -> 30.3 us  [on_device(): pl.pallas_call(functools.partial(kernel, ndp, nten), out_shape=(jax.Shape...]
where the time goes in v7:
time: 33.2 us; the launch traced here: 33 us
  Pallas kernels  32.4 us (98%)
  between operations  0.64 us (2%)
    pallas_call x1, Pallas kernels, on_device(): pl.pallas_call(functools.partial(kernel, ndp, nten), out_shape=(jax.Shape...  30.3 us
    pallas_call x1, Pallas kernels, on_device(): pl.pallas_call(hand_over, out_shape=tuple((jax.ShapeDtypeStruct(r.shape,...  2.13 us

profile of v7, /device:TPU:0, one launch (start us, length us, event | category | flops | bytes accessed | tf_op | source)
XLA Modules:
  0.0 33.0 jit_solution(3958254098446782338)
XLA Ops:
  0.6 30.3 %shard_map.95 = (bf16[512,1280]{1,0:T(8,128)(2,1)}, f32[2,16,256]{2,1,0:T(8,128)}) custom-call(s32[16]{0:T(128)} %owner_ref.1, s32[4]{0:T(128)} %block_ref.1, s32[1,512]{1,0:T(1,128)} %bitcast.3, bf16[512,1280]{1,0:T(8,128)(2,1)} %x_ref.1, bf16[512,256]{1,0:T(8,128)(2,1)} %g_ref.1, bf16[1280,1024]{1,0:T(8,128)(2,1)} %w_ref.1, bf16[2,16,1280]{2,1,0:T(8,128)(2,1)} %bitcast.2, ...), custom_call_target="tpu_custom_call" | custom-call | flops 1384120320 | bytes 5505024 | tf_op jit(solution)/shard_map/pallas_call | solution.py:411
  30.9 2.1 %shard_map.96 = (bf16[512,1280]{1,0:T(8,128)(2,1)}, f32[2,16,256]{2,1,0:T(8,128)}) custom-call(bf16[512,1280]{1,0:T(8,128)(2,1)} %get-tuple-element.4.out_ref, f32[2,16,256]{2,1,0:T(8,128)} %get-tuple-element.5.grad_ref), custom_call_target="tpu_custom_call" | custom-call | bytes 2621440 | tf_op jit(solution)/shard_map/pallas_call | solution.py:461

commit v8 on v5

--- a/solution.py
+++ b/solution.py
@@ -181,10 +181,13 @@
     for k in range(own):
         start_hops(me, k, (0, 1, 2), True)
     for i in range(nblk):
+        g_own(1, i).start()
+
+    def send_across(i):
         for j in range(1, nx):
             g_own(2 * j, i).start()
-    for i in range(nblk):
-        g_own(1, i).start()
+
+    send_across(0)
 
     local[0].wait()
     live = (tok[...] >= 0).astype(jnp.float32)
@@ -232,15 +235,18 @@
             g_wait(2 * j, i)
             g_pass(j, i).start()
 
-    if outer <= 4:
+    if outer <= nblk:
         for d in range(1, outer):
             lines(d, pass_on)
-            if d == 1:
-                near_product()
+            send_across(d)
+        for i in range(outer, nblk):
+            send_across(i)
     else:
-        near_product()
+        for i in range(1, nblk):
+            send_across(i)
         loop(1, outer, lambda d: lines(d, pass_on))
     loop(1, ndp, lambda j: to_peer(j).start())
+    near_product()
 
     for cp in local[2:]:
         cp.wait()

time: 32.3 us -> 32.4 us (level)
  no operation moved by 1% of the time
where the time goes in v8:
time: 32.4 us; the launch traced here: 32.2 us
  Pallas kernels  31.6 us (98%)
  between operations  0.64 us (2%)
    pallas_call x1, Pallas kernels, on_device(): pl.pallas_call(functools.partial(kernel, ndp, nten), out_shape=(jax.Shape...  29.5 us
    pallas_call x1, Pallas kernels, on_device(): pl.pallas_call(hand_over, out_shape=tuple((jax.ShapeDtypeStruct(r.shape,...  2.13 us

profile of v8, /device:TPU:0, one launch (start us, length us, event | category | flops | bytes accessed | tf_op | source)
XLA Modules:
  0.0 32.2 jit_solution(7457654036344086858)
XLA Ops:
  0.6 29.5 %shard_map.95 = (bf16[512,1280]{1,0:T(8,128)(2,1)}, f32[2,16,256]{2,1,0:T(8,128)}) custom-call(s32[16]{0:T(128)} %owner_ref.1, s32[4]{0:T(128)} %block_ref.1, s32[1,512]{1,0:T(1,128)} %bitcast.3, bf16[512,1280]{1,0:T(8,128)(2,1)} %x_ref.1, bf16[512,256]{1,0:T(8,128)(2,1)} %g_ref.1, bf16[1280,1024]{1,0:T(8,128)(2,1)} %w_ref.1, bf16[2,16,1280]{2,1,0:T(8,128)(2,1)} %bitcast.2, ...), custom_call_target="tpu_custom_call" | custom-call | flops 1384120320 | bytes 5505024 | tf_op jit(solution)/shard_map/pallas_call | solution.py:412
  30.1 2.1 %shard_map.96 = (bf16[512,1280]{1,0:T(8,128)(2,1)}, f32[2,16,256]{2,1,0:T(8,128)}) custom-call(bf16[512,1280]{1,0:T(8,128)(2,1)} %get-tuple-element.4.out_ref, f32[2,16,256]{2,1,0:T(8,128)} %get-tuple-element.5.grad_ref), custom_call_target="tpu_custom_call" | custom-call | bytes 2621440 | tf_op jit(solution)/shard_map/pallas_call | solution.py:462

commit v9 on v8

--- a/solution.py
+++ b/solution.py
@@ -97,26 +97,42 @@
             device_id_type=MESH,
         )
 
-    def to_peer(j):
+    def u_copy(which, j, src, dev, owner):
         return pltpu.make_async_remote_copy(
-            src_ref=u_ref,
-            dst_ref=uall.at[mine],
-            send_sem=u_send.at[j],
-            recv_sem=u_recv.at[j],
-            device_id=(lax.rem(me + j, ndp), t),
+            src_ref=src,
+            dst_ref=uall.at[pl.ds(owner * own, own)],
+            send_sem=u_send.at[which * outer + j],
+            recv_sem=u_recv.at[which * outer + j],
+            device_id=(dev, t),
             device_id_type=MESH,
         )
 
-    def from_peer(j):
-        at = pl.ds(lax.rem(me + ndp - j, ndp) * own, own)
-        pltpu.make_async_remote_copy(
-            src_ref=u_ref,
-            dst_ref=uall.at[at],
-            send_sem=u_send.at[j],
-            recv_sem=u_recv.at[j],
-            device_id=(lax.rem(me + j, ndp), t),
-            device_id_type=MESH,
-        ).wait_recv()
+    pair = inner * z + inner - 1 - y
+
+    def u_hop(which, j):
+        if which == 0:
+            src, owner = u_ref, me
+        else:
+            src, owner = uall.at[pl.ds(pair * own, own)], pair
+        dev = inner * lax.rem(z + j, outer) + y
+        return u_copy(which, j, src, dev, owner)
+
+    def u_pair():
+        return u_copy(0, 0, u_ref, pair, me)
+
+    def u_wait(which, j):
+        row = y if which == 0 else inner - 1 - y
+        owner = inner * lax.rem(z + outer - j, outer) + row
+        u_copy(which, j, u_ref, pair, owner).wait_recv()
+
+    def u_all(which, fn):
+        loop(1, outer, lambda j: fn(which, j))
+
+    def u_start(which, j):
+        u_hop(which, j).start()
+
+    def u_left(which, j):
+        u_hop(which, j).wait_send()
 
     def for_ways(fn, ways):
         for way in ways:
@@ -179,7 +195,12 @@
         ).wait_recv()
 
     for k in range(own):
-        start_hops(me, k, (0, 1, 2), True)
+        start_hops(me, k, (0, 1), True)
+        if k == 0:
+            if inner == 2:
+                u_pair().start()
+            u_all(0, u_start)
+        start_hops(me, k, (2,), True)
     for i in range(nblk):
         g_own(1, i).start()
 
@@ -235,26 +256,31 @@
             g_wait(2 * j, i)
             g_pass(j, i).start()
 
+    def u_relay():
+        if inner == 2:
+            u_copy(0, 0, u_ref, pair, pair).wait_recv()
+            u_all(1, u_start)
+
     if outer <= nblk:
+        if outer == 1:
+            u_relay()
         for d in range(1, outer):
             lines(d, pass_on)
             send_across(d)
+            if d == 1:
+                u_relay()
         for i in range(outer, nblk):
             send_across(i)
     else:
         for i in range(1, nblk):
             send_across(i)
+        u_relay()
         loop(1, outer, lambda d: lines(d, pass_on))
-    loop(1, ndp, lambda j: to_peer(j).start())
     near_product()
 
     for cp in local[2:]:
         cp.wait()
     slots = [owner[block[b]] for b in range(nblk)]
-    if inner == 2:
-        for k in range(own):
-            loop(0, outer, lambda d: got_hop(inner * d + 1 - y, k))
-
     def to_ten(which, rel):
         return pltpu.make_async_remote_copy(
             src_ref=part.at[which, 0], dst_ref=part.at[which, place_there(rel)],
@@ -269,9 +295,7 @@
             device_id=(me, ten_of(rel)), device_id_type=MESH,
         ).wait_recv()
 
-    for which, (pieces, act) in enumerate(((aall, xv), (uall, gall.at[0]))):
-        if which == 1:
-            loop(1, ndp, from_peer)
+    def send_partial(which, pieces, act):
         for b in range(nblk):
             span = slice(b * brows, (b + 1) * brows)
             part[which, 0, :, span] = lax.dot_general(
@@ -279,6 +303,16 @@
             )
         for rel in range(nten - 1, 0, -1):
             to_ten(which, rel).start()
+
+    u_all(0, u_wait)
+    if inner == 2:
+        u_all(1, u_wait)
+    send_partial(1, uall, gall.at[0])
+    if inner == 2:
+        for k in range(own):
+            loop(0, outer, lambda d: got_hop(inner * d + 1 - y, k))
+
+    send_partial(0, aall, xv)
 
     for i in range(nblk):
         pass_g(i)
@@ -357,7 +391,10 @@
     for k in range(own):
         wait_hops(me, k, (0, 1, 2), True)
     loop(1, outer, lambda d: lines(d, wait_hops))
-    loop(1, ndp, lambda j: to_peer(j).wait_send())
+    u_all(0, u_left)
+    if inner == 2:
+        u_pair().wait_send()
+        u_all(1, u_left)
     for i in range(nblk):
         for j in range(1, nx):
             g_own(2 * j, i).wait_send()

time: 32.4 us -> 33.4 us (1.031)
  Pallas kernels: 31.6 us -> 32.6 us
    pallas_call x1, Pallas kernels: 29.5 us -> 30.5 us  [on_device(): pl.pallas_call(functools.partial(kernel, ndp, nten), out_shape=(jax.Shape...]
where the time goes in v9:
time: 33.4 us; the launch traced here: 33.3 us
  Pallas kernels  32.6 us (98%)
  between operations  0.64 us (2%)
    pallas_call x1, Pallas kernels, on_device(): pl.pallas_call(functools.partial(kernel, ndp, nten), out_shape=(jax.Shape...  30.5 us
    pallas_call x1, Pallas kernels, on_device(): pl.pallas_call(hand_over, out_shape=tuple((jax.ShapeDtypeStruct(r.shape,...  2.13 us

profile of v9, /device:TPU:0, one launch (start us, length us, event | category | flops | bytes accessed | tf_op | source)
XLA Modules:
  0.0 33.3 jit_solution(2135410862936682591)
XLA Ops:
  0.6 30.5 %shard_map.95 = (bf16[512,1280]{1,0:T(8,128)(2,1)}, f32[2,16,256]{2,1,0:T(8,128)}) custom-call(s32[16]{0:T(128)} %owner_ref.1, s32[4]{0:T(128)} %block_ref.1, s32[1,512]{1,0:T(1,128)} %bitcast.3, bf16[512,1280]{1,0:T(8,128)(2,1)} %x_ref.1, bf16[512,256]{1,0:T(8,128)(2,1)} %g_ref.1, bf16[1280,1024]{1,0:T(8,128)(2,1)} %w_ref.1, bf16[2,16,1280]{2,1,0:T(8,128)(2,1)} %bitcast.2, ...), custom_call_target="tpu_custom_call" | custom-call | flops 1384120320 | bytes 5505024 | tf_op jit(solution)/shard_map/pallas_call | solution.py:449
  31.2 2.1 %shard_map.96 = (bf16[512,1280]{1,0:T(8,128)(2,1)}, f32[2,16,256]{2,1,0:T(8,128)}) custom-call(bf16[512,1280]{1,0:T(8,128)(2,1)} %get-tuple-element.4.out_ref, f32[2,16,256]{2,1,0:T(8,128)} %get-tuple-element.5.grad_ref), custom_call_target="tpu_custom_call" | custom-call | bytes 2621440 | tf_op jit(solution)/shard_map/pallas_call | solution.py:499
